TPU v7x, 128 devices: a whole 4x4x4 slice. The times are simulated.
128 devices in a mesh: grp: 16 (over z_lo, x, core), vocab: 8 (over y, z_hi).
Axes of the slice: x: 4, y: 4, z: 4 (z_hi: 2, z_lo: 2; z = z_hi * 2 + z_lo), core: 2. Of those that a mesh axis runs over, the one named last changes fastest.
Arguments:
- embedded: bfloat16 [512, 4, 5120], P('grp'), may hold values from -6 to 6
- attn_gain: float32 [5120], replicated, may hold values from 0.1 to 1.9
- query_weight: bfloat16 [5120, 4096], P(None, 'vocab'), may hold values from -0.078125 to 0.078125
- key_weight: bfloat16 [5120, 1024], P(None, 'vocab'), may hold values from -0.3125 to 0.3125
- value_weight: bfloat16 [5120, 1024], P(None, 'vocab'), may hold values from -0.078125 to 0.078125
- out_weight: bfloat16 [4096, 5120], P('vocab'), may hold values from -0.75 to 0.75
- final_gain: float32 [5120], replicated, may hold values from 0.5 to 1.5
- head_weight: bfloat16 [5120, 81920], P(None, ('grp', 'vocab')), may hold values from -3 to 3
- prefix_keys: bfloat16 [16, 8, 2048, 128], P('grp', 'vocab'), may hold values from -150 to 150
- prefix_values: bfloat16 [16, 8, 2048, 128], P('grp', 'vocab'), may hold values from -6 to 6
- sample_prompt: int32 [512], P('grp'), may hold values from 0 to 15, as said below
Outputs:
- log_probs: float32 [512, 4, 81920], P(None, None, ('grp', 'vocab'))
Inputs may be any that keep to these rules, and one draw needn't show every extreme that they name: `sample_prompt`: each device's aligned block of 32 samples holds exactly 2 samples of every one of the 16 prompts, in a drawn order.
All inputs are finite; a program needn't handle non-finite values.
Results may differ from a plain program's by a relative error of at most 0.0029.
The roundings to bfloat16 on the way count: a program that leaves them out, or rounds other values in their place, can miss the bound.
Values may be sent and summed in bfloat16 or wider, within the bound.
No kernel may reach another device: no remote copies, remote signals or barrier semaphores. Data moves between devices by JAX's collectives and lax.ppermute only.
A program may use at most 128 MiB of HBM per device.

v0:
```python
import jax
import jax.numpy as jnp
from jax import lax
from jax.sharding import PartitionSpec as P


def combined_all(part, axis, combine):
    gathered = jax.tree.map(lambda a: lax.all_gather(a, axis), part)

    def take(source):
        return jax.tree.map(lambda a: lax.dynamic_index_in_dim(a, source, 0, False), gathered)

    return lax.fori_loop(
        1, lax.axis_size(axis), lambda source, state: combine(state, take(source)), take(0)
    )


def rms_scale(rows, gain):
    mean_sq = jnp.mean(rows * rows, axis=-1, keepdims=True)
    return rows * lax.rsqrt(mean_sq + 1e-06) * gain


def softmax_parts(scores, value_rows, value_form):
    peaks = jnp.max(scores, axis=-1)
    powers = jnp.exp(scores - peaks[..., None])
    totals = jnp.sum(powers, axis=-1)
    weighted = jnp.einsum(
        value_form, powers.astype(jnp.bfloat16), value_rows, preferred_element_type=jnp.float32
    )
    return (peaks, totals, weighted)


def on_device(
    embedded,
    attn_gain,
    query_weight,
    key_weight,
    value_weight,
    out_weight,
    final_gain,
    head_weight,
    prefix_keys,
    prefix_values,
    sample_prompt,
):
    sample_count, step_count, model_width = embedded.shape
    heads_here = prefix_keys.shape[1]
    head_size = prefix_keys.shape[3]
    groups = query_weight.shape[1] // (heads_here * head_size)
    prompts = lax.axis_size("grp")
    per_prompt = sample_count // prompts
    score_scale = 1.0 / head_size**0.5
    flat_rows = embedded.reshape(sample_count * step_count, model_width)
    normed_input = rms_scale(flat_rows.astype(jnp.float32), attn_gain).astype(jnp.bfloat16)
    queries = jnp.dot(normed_input, query_weight, preferred_element_type=jnp.float32).astype(
        jnp.bfloat16
    )
    queries = queries.reshape(sample_count, step_count, heads_here, groups, head_size)
    new_keys = jnp.dot(normed_input, key_weight, preferred_element_type=jnp.float32).astype(
        jnp.bfloat16
    )
    new_keys = new_keys.reshape(sample_count, step_count, heads_here, head_size)
    new_values = jnp.dot(normed_input, value_weight, preferred_element_type=jnp.float32).astype(
        jnp.bfloat16
    )
    new_values = new_values.reshape(sample_count, step_count, heads_here, head_size)
    ordering = jnp.argsort(sample_prompt, stable=True)
    restore = jnp.argsort(ordering, stable=True)
    sorted_queries = jnp.take(queries, ordering, axis=0)
    sorted_queries = sorted_queries.reshape(
        prompts, per_prompt, step_count, heads_here, groups, head_size
    )
    scores = (
        jnp.einsum(
            "nptjgh,njlh->nptjgl",
            sorted_queries,
            lax.all_gather(prefix_keys, "grp", axis=0, tiled=True),
            preferred_element_type=jnp.float32,
        )
        * score_scale
    )
    partials = softmax_parts(
        scores, lax.all_gather(prefix_values, "grp", axis=0, tiled=True), "nptjgl,njlh->nptjgh"
    )
    prefix_peak, prefix_total, prefix_sum = tuple((fresh for fresh in partials))
    prefix_peak = jnp.take(
        prefix_peak.reshape(sample_count, step_count, heads_here, groups), restore, axis=0
    )
    prefix_total = jnp.take(
        prefix_total.reshape(sample_count, step_count, heads_here, groups), restore, axis=0
    )
    prefix_sum = jnp.take(
        prefix_sum.reshape(sample_count, step_count, heads_here, groups, head_size), restore, axis=0
    )
    scores = (
        jnp.einsum("stjgh,sujh->stjgu", queries, new_keys, preferred_element_type=jnp.float32)
        * score_scale
    )
    step_index = jnp.arange(step_count)
    causal = step_index[:, None] >= step_index[None, :]
    scores = jnp.where(causal[None, :, None, None, :], scores, -1e30)
    new_peak, new_total, new_sum = softmax_parts(scores, new_values, "stjgu,sujh->stjgh")
    joint_peak = jnp.maximum(prefix_peak, new_peak)
    prefix_factor = jnp.exp(prefix_peak - joint_peak)
    new_factor = jnp.exp(new_peak - joint_peak)
    numerator = prefix_sum * prefix_factor[..., None] + new_sum * new_factor[..., None]
    denominator = prefix_total * prefix_factor + new_total * new_factor
    attended = (numerator / denominator[..., None]).astype(jnp.bfloat16)
    attended = attended.reshape(sample_count * step_count, heads_here * groups * head_size)
    partial_heads = jnp.dot(attended, out_weight, preferred_element_type=jnp.float32)
    summed = lax.psum(partial_heads, "vocab")
    normed = rms_scale(flat_rows.astype(jnp.float32) + summed, final_gain).astype(jnp.bfloat16)
    logits = jnp.dot(
        lax.all_gather(normed, "grp", axis=0, tiled=True),
        head_weight,
        preferred_element_type=jnp.float32,
    )
    peaks = jnp.max(logits, axis=-1, keepdims=True)
    masses = jnp.sum(jnp.exp(logits - peaks), axis=-1, keepdims=True)

    def combine(left_part, right_part):
        larger = jnp.maximum(left_part[0], right_part[0])
        return (
            larger,
            left_part[1] * jnp.exp(left_part[0] - larger)
            + right_part[1] * jnp.exp(right_part[0] - larger),
        )

    peak_all, mass_all = combined_all((peaks, masses), ("grp", "vocab"), combine)
    log_probs = logits - (peak_all + jnp.log(mass_all))
    return log_probs.reshape(-1, step_count, head_weight.shape[1])


def solution(mesh):
    placed = (
        P("grp", None, None),
        P(),
        P(None, "vocab"),
        P(None, "vocab"),
        P(None, "vocab"),
        P("vocab", None),
        P(),
        P(None, ("grp", "vocab")),
        P("grp", "vocab", None, None),
        P("grp", "vocab", None, None),
        P("grp"),
    )
    return jax.shard_map(
        on_device,
        mesh=mesh,
        in_specs=placed,
        out_specs=P(None, None, ("grp", "vocab")),
        check_vma=False,
    )
```

profile of v0, /device:TPU:1, one launch (start us, length us, event | category | flops | bytes accessed | tf_op | source)
XLA Modules:
  0.0 1111.2 jit_solution(4127521570594959980)
XLA Ops:
  8.1 3.3 reshape.176
  12.2 2.1 multiply_convert_fusion.1
  14.3 3.3 convolution_convert_fusion
  17.7 1.6 sort.31
  19.5 1.6 sort.32
  22.3 1.3 fusion.41
  23.8 1.8 convolution_convert_fusion.1
  25.7 39.6 %all-gather.8.cloned.1.call-done = bf16[16,1,2048,128]{3,2,1,0:T(8,128)(2,1)} async-done(((bf16[1,1,2048,128]{3,2,1,0:T(8,128)(2,1)}), bf16[16,1,2048,128]{3,2,1,0:T(8,128)(2,1)}) %all-gather.8.cloned.1.call-update) | async-done | bytes 8388624 | tf_op jit(solution)/shard_map/all_gather | solution.py:77
  65.3 6.4 bitcast_reduce_fusion
  71.7 2.0 copy-done.2
  73.7 2.0 fusion.7
  76.9 42.7 %all-gather.10.cloned.1.call-done = bf16[16,1,2048,128]{3,2,1,0:T(8,128)(2,1)} async-done(((bf16[1,1,2048,128]{3,2,1,0:T(8,128)(2,1)}), bf16[16,1,2048,128]{3,2,1,0:T(8,128)(2,1)}) %all-gather.10.cloned.1.call-update) | async-done | bytes 8388624 | tf_op jit(solution)/shard_map/all_gather | solution.py:83
  119.6 7.5 fusion.2
  128.7 4.8 fusion.25
  133.8 126.5 %all-reduce.2.cloned.1.call-done = f32[128,5120]{1,0:T(8,128)} async-done(((f32[128,5120]{1,0:T(8,128)}), f32[128,5120]{1,0:T(8,128)}) %all-reduce.2.cloned.1.call-update) | async-done | bytes 2621456 | tf_op jit(solution)/shard_map/psum | solution.py:111
  260.3 3.0 multiply_reduce_fusion
  263.3 1.4 multiply_convert_fusion
  264.7 114.7 %all-gather.12.cloned.1.call-done = bf16[2048,5120]{1,0:T(8,128)(2,1)} async-done(((bf16[128,5120]{1,0:T(8,128)(2,1)}), bf16[2048,5120]{1,0:T(8,128)(2,1)}) %all-gather.12.cloned.1.call-update) | async-done | bytes 20971536 | tf_op jit(solution)/shard_map/all_gather | solution.py:114
  379.5 22.6 %fusion.42 = (f32[2048]{0:T(1024)S(1)}, f32[2048,640]{1,0:T(8,128)}) fusion(bf16[2048,5120]{1,0:T(8,128)(2,1)} %all-gather.12.cloned.1.call-done, bf16[5120,640]{1,0:T(8,128)(2,1)} %param.22), kind=kOutput, calls=%fused_computation.77 | convolution fusion | flops 13423081472 | bytes 32776192 | tf_op jit(solution)/shard_map/dot_general | solution.py:113
  402.1 4.3 exponential_reduce_fusion
  407.0 291.6 %all-gather.16.cloned.1.call-done = f32[262144]{0:T(1024)} async-done(((f32[2048]{0:T(1024)}), f32[262144]{0:T(1024)}) %all-gather.16.cloned.1.call-update) | async-done | bytes 1048592 | tf_op jit(solution)/shard_map/all_gather | solution.py:8
  699.3 293.2 %all-gather.14.cloned.1.call-done = f32[262144]{0:T(1024)} async-done(((f32[2048]{0:T(1024)}), f32[262144]{0:T(1024)}) %all-gather.14.cloned.1.call-update) | async-done | bytes 1048592 | tf_op jit(solution)/shard_map/all_gather | solution.py:8
  993.2 98.7 %while.17 = (s32[]{:T(128)}, f32[2048,1]{0,1:T(1,128)S(1)}, f32[2048,1]{0,1:T(1,128)S(1)}, f32[128,2048,1]{1,2,0:T(1,128)}, f32[128,2048,1]{1,2,0:T(1,128)}, /*index=5*/s32[]{:T(128)}, s32[]{:T(128)}, s32[]{:T(128)}) while((s32[]{:T(128)}, f32[2048,1]{0,1:T(1,128)S(1)}, f32[2048,1]{0,1:T(1,128)S(1)}, f32[128,2048,1]{1,2,0:T(1,128)}, ...), condition=%wide.region_12.14_spmd, body=%wide.region_11.13_spmd.sunk | while | flops 12293 | bytes 49283 | solution.py:13
  999.4 0.8 fusion.56
  1000.2 0.8 fusion.56
  1008.0 0.8 fusion.56
  1010.3 0.8 fusion.56
  1030.5 0.8 fusion.56
  1045.3 0.8 fusion.56
  1081.8 0.8 fusion.56
  1092.0 5.3 broadcast_subtract_fusion
  1097.3 7.1 reshape.175
  (173 shorter events, 100.5 us)
Async XLA Ops:
  6.5 15.3 %copy-start = (bf16[5120,128]{1,0:T(8,128)(2,1)S(1)}, bf16[5120,128]{1,0:T(8,128)(2,1)}, u32[]{:S(2)}) copy-start(bf16[5120,128]{1,0:T(8,128)(2,1)} %param.18) | copy-start | bytes 3932164
  6.5 4.8 copy-start.3
  6.5 5.7 copy-start.5
  6.5 58.7 %all-gather.8.cloned.1.call-start = ((), (), s32[]{:S(2)}) async-start(), calls=%async_computation | async-start | bytes 8912896 | tf_op jit(solution)/shard_map/all_gather | solution.py:77
  7.3 112.4 %all-gather.10.cloned.1.call-start = ((), (), s32[]{:S(2)}) async-start(), calls=%async_computation.1 | async-start | bytes 8912896 | tf_op jit(solution)/shard_map/all_gather | solution.py:83
  8.0 252.3 %all-reduce.2.cloned.1.call-start = ((), (), s32[]{:S(2)}) async-start(), calls=%async_computation.2 | async-start | bytes 5242880 | tf_op jit(solution)/shard_map/psum | solution.py:111
  14.3 3.4 copy-start.7
  71.7 2.0 copy-start.2
  133.6 129.7 %copy-start.6 = (f32[5120]{0:T(1024)S(1)}, f32[5120]{0:T(1024)}, u32[]{:S(2)}) copy-start(f32[5120]{0:T(1024)} %param.21) | copy-start | bytes 61444
  133.6 245.9 %all-gather.12.cloned.1.call-start = ((), (), s32[]{:S(2)}) async-start(), calls=%async_computation.3 | async-start | bytes 22282240 | tf_op jit(solution)/shard_map/all_gather | solution.py:114
  264.7 433.9 %all-gather.16.cloned.1.call-start = ((), (), s32[]{:S(2)}) async-start(), calls=%async_computation.5 | async-start | bytes 1056768 | tf_op jit(solution)/shard_map/all_gather | solution.py:8
  402.1 4.4 copy-start.4
  406.5 586.0 %all-gather.14.cloned.1.call-start = ((), (), s32[]{:S(2)}) async-start(), calls=%async_computation.4 | async-start | bytes 1056768 | tf_op jit(solution)/shard_map/all_gather | solution.py:8
  1092.0 12.4 %copy-start.1 = (bf16[5120,128]{1,0:T(8,128)(2,1)S(1)}, bf16[5120,128]{1,0:T(8,128)(2,1)}, u32[]{:S(2)}) copy-start(bf16[5120,128]{1,0:T(8,128)(2,1)} %param.18) | copy-start | bytes 3932164
Sparse Core Ops, SparseCore 0:
  9.1 56.1 all-gather.7
  67.0 52.6 all-gather.9
  133.7 126.5 all-reduce.1
  264.8 114.6 all-gather.11
  406.6 291.9 all-gather.15
  700.2 292.2 all-gather.13
where the time goes:
time: 1130 us; the launch traced here: 1110 us
  waiting for transfers between devices  910 us (81%)
  other arithmetic  119 us (11%)
  matrix products  49 us (4%)
  local copies, waits for them, and re-layouts  16.7 us (1%)
  between operations  13.7 us (1%)
    all_gather x2, waiting for transfers between devices, combined_all(): gathered = jax.tree.map(lambda a: lax.all_gather(a, axis), part)  585 us
    psum x1, waiting for transfers between devices, on_device(): summed = lax.psum(partial_heads, 'vocab')  126 us
    all_gather x1, waiting for transfers between devices, on_device(): lax.all_gather(normed, 'grp', axis=0, tiled=True)  115 us
    add x127, other arithmetic, combine(): left_part[1] * jnp.exp(left_part[0] - larger)  96.9 us
    all_gather x1, waiting for transfers between devices, on_device(): lax.all_gather(prefix_values, 'grp', axis=0, tiled=True)  42.7 us
    all_gather x1, waiting for transfers between devices, on_device(): lax.all_gather(prefix_keys, 'grp', axis=0, tiled=True)  39.6 us
    dot_general x1, matrix products, on_device(): jnp.dot(lax.all_gather(normed, 'grp', axis=0, tiled=True), head_weight, p...  22.6 us
  transfers between devices with their start and end apart: 6, of which 6 were waited for; matrix products, arithmetic and copies ran while one was open for 2% of the time, Pallas kernels for 0%

commit v1 on v0

v1 whole, which is shorter than its diff:
```python
import jax
import jax.numpy as jnp
import numpy as np
from jax import lax
from jax.sharding import PartitionSpec as P

BOTH = ("grp", "vocab")
RING = 4
PIECES = ((0, 1664), (1664, 3456), (3456, 5120))
ORDERS = ("xyz", "yzx", "zxy")


def place_of(flat):
    grp, vocab = divmod(flat, 8)
    z_lo, rest = divmod(grp, 8)
    x, core = divmod(rest, 2)
    y, z_hi = divmod(vocab, 2)
    return {"x": x, "y": y, "z": z_hi * 2 + z_lo, "core": core}


def flat_of(at):
    grp = (at["z"] % 2) * 8 + at["x"] * 2 + at["core"]
    return grp * 8 + at["y"] * 2 + at["z"] // 2


def ring_pairs(axis):
    pairs = []
    for source in range(128):
        at = place_of(source)
        at[axis] = (at[axis] + (1 if at["core"] == 0 else -1)) % RING
        pairs.append((source, flat_of(at)))
    return pairs


def core_pairs():
    pairs = []
    for source in range(128):
        at = place_of(source)
        at["core"] = 1 - at["core"]
        pairs.append((source, flat_of(at)))
    return pairs


STEP = {axis: ring_pairs(axis) for axis in "xyz"}
SWAP = core_pairs()


def swap_cores(block):
    return lax.ppermute(block, BOTH, SWAP)


def ring_gather(blocks):
    held = list(blocks)
    for stage in range(3):
        rounds = [[part] for part in held]
        for _ in range(RING - 1):
            for k, order in enumerate(ORDERS):
                rounds[k].append(lax.ppermute(rounds[k][-1], BOTH, STEP[order[stage]]))
        held = [jnp.stack(parts) for parts in rounds]
    return held


def rms_scale(rows, gain):
    mean_sq = jnp.mean(rows * rows, axis=-1, keepdims=True)
    return rows * lax.rsqrt(mean_sq + 1e-06) * gain


def softmax_parts(scores, value_rows, value_form):
    peaks = jnp.max(scores, axis=-1)
    powers = jnp.exp(scores - peaks[..., None])
    totals = jnp.sum(powers, axis=-1)
    weighted = jnp.einsum(
        value_form, powers.astype(jnp.bfloat16), value_rows, preferred_element_type=jnp.float32
    )
    return (peaks, totals, weighted)


def log_sum(values, axis):
    top = jnp.max(values, axis=axis, keepdims=True)
    return jnp.squeeze(top, axis) + jnp.log(jnp.sum(jnp.exp(values - top), axis=axis))


def spread(values, axis):
    copies = lax.axis_size(axis)
    return lax.all_to_all(
        jnp.broadcast_to(values[None], (copies,) + values.shape), axis, 0, 0, tiled=True
    )


def on_device(
    embedded,
    attn_gain,
    query_weight,
    key_weight,
    value_weight,
    out_weight,
    final_gain,
    head_weight,
    prefix_keys,
    prefix_values,
    sample_prompt,
):
    samples, steps, width = embedded.shape
    head = prefix_keys.shape[3]
    groups = query_weight.shape[1] // head
    rows = samples * steps
    scale = 1.0 / head**0.5
    other_weight = swap_cores(head_weight)

    flat_rows = embedded.reshape(rows, width)
    normed_input = rms_scale(flat_rows.astype(jnp.float32), attn_gain).astype(jnp.bfloat16)
    project = lambda w: jnp.dot(normed_input, w, preferred_element_type=jnp.float32).astype(
        jnp.bfloat16
    )
    projected = jnp.concatenate(
        [project(query_weight), project(key_weight), project(value_weight)], axis=1
    )

    same = sample_prompt[:, None] == sample_prompt[None, :]
    earlier = jnp.arange(samples)[:, None] > jnp.arange(samples)[None, :]
    slot = sample_prompt * 2 + jnp.sum(same & earlier, axis=1, dtype=jnp.int32)
    row_slot = (slot[:, None] * steps + jnp.arange(steps, dtype=jnp.int32)[None, :]).reshape(rows)
    to_sorted = (row_slot[None, :] == jnp.arange(rows, dtype=jnp.int32)[:, None]).astype(jnp.bfloat16)
    sorted_rows = jnp.dot(to_sorted, projected, preferred_element_type=jnp.float32).astype(
        jnp.bfloat16
    )
    local = lax.all_to_all(sorted_rows, "grp", 0, 0, tiled=True)

    cut = groups * head
    queries = local[:, :cut].reshape(samples, steps, groups, head)
    new_keys = local[:, cut : cut + head].reshape(samples, steps, head)
    new_values = local[:, cut + head :].reshape(samples, steps, head)
    scores = (
        jnp.einsum("stgh,lh->stgl", queries, prefix_keys[0, 0], preferred_element_type=jnp.float32)
        * scale
    )
    prefix_peak, prefix_total, prefix_sum = softmax_parts(
        scores, prefix_values[0, 0], "stgl,lh->stgh"
    )
    scores = jnp.einsum("stgh,suh->stgu", queries, new_keys, preferred_element_type=jnp.float32) * scale
    step_index = jnp.arange(steps)
    causal = step_index[:, None] >= step_index[None, :]
    scores = jnp.where(causal[None, :, None, :], scores, -1e30)
    new_peak, new_total, new_sum = softmax_parts(scores, new_values, "stgu,suh->stgh")
    peak = jnp.maximum(prefix_peak, new_peak)
    prefix_factor = jnp.exp(prefix_peak - peak)
    new_factor = jnp.exp(new_peak - peak)
    numerator = prefix_sum * prefix_factor[..., None] + new_sum * new_factor[..., None]
    denominator = prefix_total * prefix_factor + new_total * new_factor
    attended = (numerator / denominator[..., None]).astype(jnp.bfloat16).reshape(rows, cut)

    back = lax.all_to_all(attended, "grp", 0, 0, tiled=True)
    attended = jnp.dot(to_sorted.T, back, preferred_element_type=jnp.float32).astype(jnp.bfloat16)
    partial_heads = jnp.dot(attended, out_weight, preferred_element_type=jnp.float32)
    shares = lax.axis_size("vocab")
    mine = rows // shares
    arrived = lax.all_to_all(partial_heads, "vocab", 0, 0, tiled=True)
    summed = jnp.sum(arrived.reshape(shares, mine, width), axis=0)
    own_rows = lax.dynamic_slice_in_dim(flat_rows, lax.axis_index("vocab") * mine, mine, 0)
    normed = rms_scale(own_rows.astype(jnp.float32) + summed, final_gain).astype(jnp.bfloat16)

    gathered = ring_gather([normed[:, a:b] for a, b in PIECES])
    turned = (
        gathered[0],
        gathered[1].transpose(1, 2, 0, 3, 4),
        gathered[2].transpose(2, 0, 1, 3, 4),
    )
    plane = jnp.concatenate([t.reshape(64 * mine, t.shape[-1]) for t in turned], axis=1)
    logits = jnp.dot(plane, head_weight, preferred_element_type=jnp.float32)
    other_logits = jnp.dot(plane, other_weight, preferred_element_type=jnp.float32)
    crossed = swap_cores(other_logits)

    core = lax.axis_index("grp") % 2
    z = (lax.axis_index("vocab") % 2) * 2 + lax.axis_index("grp") // 8
    y = lax.axis_index("vocab") // 2
    x = (lax.axis_index("grp") // 2) % 4
    places = jnp.arange(4, dtype=jnp.int32)
    near = lambda c, at: jnp.where(c == 0, at - places, places - at) % 4
    find = lambda c: (
        near(c, z)[:, None, None] * 16 + near(c, y)[None, :, None] * 4 + near(c, x)[None, None, :]
    )

    local_sum = log_sum(jnp.concatenate([logits, other_logits], axis=1), 1)
    mine_order = find(core).reshape(64)
    local_sum = jnp.take(local_sum.reshape(64, mine), mine_order, axis=0)
    over_grp = spread(local_sum, "grp").reshape(8, 2, 64, mine)
    over_grp = log_sum(over_grp, 0)
    total = log_sum(spread(over_grp, "vocab").reshape(shares, 2, 64, mine), 0)

    def rearrange(blocks):
        return blocks.transpose((2, 4, 0, 3, 1) + tuple(range(5, blocks.ndim)))

    total = rearrange(total.reshape(2, 2, 2, 4, 4, mine))
    own_at = find(core).reshape(64)
    other_at = find(1 - core).reshape(64) + 64
    first = jnp.where(core == 0, own_at, other_at)
    second = jnp.where(core == 0, other_at, own_at)
    source = rearrange(jnp.stack([first, second]).reshape(2, 2, 2, 4, 4)).reshape(128)
    blocks = jnp.concatenate([logits, crossed]).reshape(128, mine, head_weight.shape[1])
    result = jnp.take(blocks, source, axis=0) - total.reshape(128, mine, 1)
    return result.reshape(-1, steps, head_weight.shape[1])


def solution(mesh):
    placed = (
        P("grp", None, None),
        P(),
        P(None, "vocab"),
        P(None, "vocab"),
        P(None, "vocab"),
        P("vocab", None),
        P(),
        P(None, ("grp", "vocab")),
        P("grp", "vocab", None, None),
        P("grp", "vocab", None, None),
        P("grp"),
    )
    return jax.shard_map(
        on_device,
        mesh=mesh,
        in_specs=placed,
        out_specs=P(None, None, ("grp", "vocab")),
        check_vma=False,
    )
```

time: 1130 us -> 275 us (0.24); the launches traced: 1110 us -> 273 us
  waiting for transfers between devices: 910 us -> 79.8 us
  other arithmetic: 119 us -> 39.1 us
  starting transfers between devices: 0.38 us -> 76.3 us
  between operations: 13.7 us -> 0.39 us
  local copies, waits for them, and re-layouts: 16.7 us -> 28.6 us
    all_gather x5 -> x0, waiting for transfers between devices: 782 us -> none  [the longest x2 585 us: combined_all(): gathered = jax.tree.map(lambda a: lax.all_gather(a, axis), part)]
    psum x1 -> x0, waiting for transfers between devices: 126 us -> none  [on_device(): summed = lax.psum(partial_heads, 'vocab')]
    add x128 -> x9, other arithmetic: 96.9 us -> 0.41 us  [the longest x4 0.29 us: on_device(): near(c, z)[:, None, None] * 16 + near(c, y)[None, :, None] * 4]
    all_to_all x0 -> x4, waiting for transfers between devices: none -> 56 us  [the longest x1 37.2 us: on_device(): arrived = lax.all_to_all(partial_heads, 'vocab', 0, 0, tiled=True)]
    ppermute x0 -> x29, starting transfers between devices: none -> 54.4 us  [the longest x27 39.9 us: ring_gather(): rounds[k].append(lax.ppermute(rounds[k][-1], BOTH, STEP[order[stage]]))]
    ppermute x0 -> x29, waiting for transfers between devices: none -> 23.8 us  [the longest x27 23.8 us: ring_gather(): rounds[k].append(lax.ppermute(rounds[k][-1], BOTH, STEP[order[stage]]))]
    all_to_all x0 -> x4, starting transfers between devices: none -> 22 us  [the longest x2 7.47 us: spread(): lax.all_to_all(jnp.broadcast_to(values[None], (copies,) + values.shape),...]
    dot_general x6 -> x8, matrix products: 36 us -> 34.1 us  [the longest x1 12.8 us: on_device(): jnp.dot(plane, other_weight, preferred_element_type=jnp.float32)]
  transfers between devices with their start and end apart: 6 -> 33, of which waited for: 6 -> 17; matrix products, arithmetic and copies ran while one was open for 2% -> 14% of each run, Pallas kernels for 0% -> 0%
where the time goes in v1:
time: 275 us; the launch traced here: 273 us
  waiting for transfers between devices  79.8 us (29%)
  starting transfers between devices  76.3 us (28%)
  matrix products  40.1 us (15%)
  other arithmetic  39.1 us (14%)
  local copies, waits for them, and re-layouts  28.6 us (10%)
  blocking collectives  9.11 us (3%)
    ppermute x27, starting transfers between devices, ring_gather(): rounds[k].append(lax.ppermute(rounds[k][-1], BOTH, STEP[order[stage]]))  39.9 us
    all_to_all x1, waiting for transfers between devices, on_device(): arrived = lax.all_to_all(partial_heads, 'vocab', 0, 0, tiled=True)  37.2 us
    ppermute x27, waiting for transfers between devices, ring_gather(): rounds[k].append(lax.ppermute(rounds[k][-1], BOTH, STEP[order[stage]]))  23.8 us
    ppermute x2, starting transfers between devices, swap_cores(): return lax.ppermute(block, BOTH, SWAP)  14.5 us
    gather x2, local copies, waits for them, and re-layouts, on_device(): result = jnp.take(blocks, source, axis=0) - total.reshape(128, mine, 1)  12.9 us
    dot_general x1, matrix products, on_device(): jnp.dot(plane, other_weight, preferred_element_type=jnp.float32)  12.8 us
    dot_general x1, matrix products, on_device(): logits = jnp.dot(plane, head_weight, preferred_element_type=jnp.float32)  12.8 us
    all_to_all x2, waiting for transfers between devices, spread(): lax.all_to_all(jnp.broadcast_to(values[None], (copies,) + values.shape),...  12.1 us
  transfers between devices with their start and end apart: 33, of which 17 were waited for; matrix products, arithmetic and copies ran while one was open for 14% of the time, Pallas kernels for 0%

profile of v1, /device:TPU:1, one launch (start us, length us, event | category | flops | bytes accessed | tf_op | source)
XLA Modules:
  0.0 273.5 jit_solution(2215256528203959425)
XLA Ops:
  9.9 7.2 %all-to-all-start = ((bf16[16,8,768]{2,1,0:T(8,128)(2,1)}), bf16[16,8,768]{2,1,0:T(8,128)(2,1)S(1)}, u32[]{:S(2)}, u32[]{:S(2)}) async-start(bf16[16,8,768]{2,1,0:T(8,128)(2,1)} %fusion.16), calls=%async_computation | async-start | bytes 393216 | tf_op jit(solution)/shard_map/all_to_all | solution.py:127
  17.0 6.6 %all-to-all-done = bf16[16,8,768]{2,1,0:T(8,128)(2,1)S(1)} async-done(((bf16[16,8,768]{2,1,0:T(8,128)(2,1)}), bf16[16,8,768]{2,1,0:T(8,128)(2,1)S(1)}, u32[]{:S(2)}, u32[]{:S(2)}) %all-to-all-start) | async-done | bytes 196640 | tf_op jit(solution)/shard_map/all_to_all | solution.py:127
  23.8 2.7 multiply_reduce_fusion
  28.6 3.2 %fusion.4 = f32[32,4,4]{0,2,1:T(4,128)S(1)} fusion(f32[32,4,4,2048]{3,0,2,1:T(8,128)} %get-tuple-element.33, f32[32,4,4]{0,2,1:T(4,128)S(1)} %get-tuple-element.32), kind=kLoop, calls=%fused_computation.13 | loop fusion | flops 3145216 | bytes 4198400 | tf_op jit(solution)/shard_map/reduce_sum | solution.py:71
  32.9 9.1 %all_to_all.43 = bf16[16,8,512]{2,1,0:T(8,128)(2,1)S(1)} all-to-all(bf16[16,8,512]{2,1,0:T(8,128)(2,1)S(1)} %all_to_all.31), channel_id=1, replica_groups=mesh['grp'=16,'vocab'=8] {'grp'}, dimensions={0} | all-to-all | bytes 262144 | tf_op jit(solution)/shard_map/all_to_all | solution.py:152
  42.0 5.0 %fusion.17 = f32[128,5120]{1,0:T(8,128)} fusion(bf16[512,5120]{1,0:T(8,128)(2,1)} %param.16, bf16[16,8,512]{2,1,0:T(8,128)(2,1)S(1)} %all_to_all.43, s32[128]{0:T(128)S(1)} %add.384), kind=kOutput, calls=%fused_computation.28 | convolution fusion | flops 687947776 | bytes 7995904 | tf_op jit(solution)/shard_map/dot_general | solution.py:154
  47.0 7.3 %all-to-all-start.2 = ((f32[8,16,5120]{2,1,0:T(8,128)}), f32[8,16,5120]{2,1,0:T(8,128)}, u32[]{:S(2)}, u32[]{:S(2)}) async-start(f32[8,16,5120]{2,1,0:T(8,128)} %bitcast.129), calls=%async_computation.2 | async-start | bytes 5242880 | tf_op jit(solution)/shard_map/all_to_all | solution.py:157
  55.1 37.2 %all-to-all-done.2 = f32[8,16,5120]{2,1,0:T(8,128)} async-done(((f32[8,16,5120]{2,1,0:T(8,128)}), f32[8,16,5120]{2,1,0:T(8,128)}, u32[]{:S(2)}, u32[]{:S(2)}) %all-to-all-start.2) | async-done | bytes 2621472 | tf_op jit(solution)/shard_map/all_to_all | solution.py:157
  106.6 2.9 %collective-permute-done.11 = bf16[16,1792]{1,0:T(8,128)(2,1)S(1)} collective-permute-done((bf16[16,1792]{1,0:T(8,128)(2,1)S(1)}, bf16[16,1792]{1,0:T(8,128)(2,1)S(1)}, u32[]{:S(2)}, u32[]{:S(2)}) %collective-permute-start.11) | collective-permute-done | bytes 57376 | tf_op jit(solution)/shard_map/ppermute | solution.py:58
  118.8 2.8 %collective-permute-done.4 = bf16[4,16,1664]{2,1,0:T(8,128)(2,1)S(1)} collective-permute-done((bf16[4,16,1664]{2,1,0:T(8,128)(2,1)S(1)}, bf16[4,16,1664]{2,1,0:T(8,128)(2,1)S(1)}, u32[]{:S(2)}, u32[]{:S(2)}) %collective-permute-start.4) | collective-permute-done | bytes 213024 | tf_op jit(solution)/shard_map/ppermute | solution.py:58
  121.6 3.0 %collective-permute-start.5 = (bf16[4,16,1664]{2,1,0:T(8,128)(2,1)S(1)}, bf16[4,16,1664]{2,1,0:T(8,128)(2,1)S(1)}, u32[]{:S(2)}, u32[]{:S(2)}) collective-permute-start(bf16[4,16,1664]{2,1,0:T(8,128)(2,1)S(1)} %collective-permute-done.4), channel_id=1, source_target_pairs={{0,2},{1,3},{2,4},{3,5},{4,6},{5,7},{6,0},{7,1},{8,14},{9,15},{10,... | collective-permute-start | bytes 638984 | tf_op jit(solution)/shard_map/ppermute | solution.py:58
  132.6 5.0 %collective-permute-done.24 = bf16[4,4,16,1664]{3,2,1,0:T(8,128)(2,1)} collective-permute-done((bf16[4,4,16,1664]{3,2,1,0:T(8,128)(2,1)}, bf16[4,4,16,1664]{3,2,1,0:T(8,128)(2,1)}, u32[]{:S(2)}, u32[]{:S(2)}) %collective-permute-start.24) | collective-permute-done | bytes 852000 | tf_op jit(solution)/shard_map/ppermute | solution.py:58
  143.5 2.8 %collective-permute-start.16 = (bf16[4,4,16,1792]{3,2,1,0:T(8,128)(2,1)}, bf16[4,4,16,1792]{3,2,1,0:T(8,128)(2,1)}, u32[]{:S(2)}, u32[]{:S(2)}) collective-permute-start(bf16[4,4,16,1792]{3,2,1,0:T(8,128)(2,1)} %collective-permute-done.15), channel_id=1, source_target_pairs={{0,16},{1,17},{2,18},{3,19},{4,20},{5,21},{6,22},{7,23},{8,56},{9,... | collective-permute-start | bytes 2752520 | tf_op jit(solution)/shard_map/ppermute | solution.py:58
  146.4 3.3 %collective-permute-done.25 = bf16[4,4,16,1664]{3,2,1,0:T(8,128)(2,1)} collective-permute-done((bf16[4,4,16,1664]{3,2,1,0:T(8,128)(2,1)}, bf16[4,4,16,1664]{3,2,1,0:T(8,128)(2,1)}, u32[]{:S(2)}, u32[]{:S(2)}) %collective-permute-start.25) | collective-permute-done | bytes 852000 | tf_op jit(solution)/shard_map/ppermute | solution.py:58
  149.8 3.4 %collective-permute-start.26 = (bf16[4,4,16,1664]{3,2,1,0:T(8,128)(2,1)}, bf16[4,4,16,1664]{3,2,1,0:T(8,128)(2,1)}, u32[]{:S(2)}, u32[]{:S(2)}) collective-permute-start(bf16[4,4,16,1664]{3,2,1,0:T(8,128)(2,1)} %collective-permute-done.25), channel_id=1, source_target_pairs={{0,2},{1,3},{2,4},{3,5},{4,6},{5,7},{6,0},{7,1},{8,14},{9,15},{10,... | collective-permute-start | bytes 2555912 | tf_op jit(solution)/shard_map/ppermute | solution.py:58
  156.9 3.4 %collective-permute-start.17 = (bf16[4,4,16,1792]{3,2,1,0:T(8,128)(2,1)}, bf16[4,4,16,1792]{3,2,1,0:T(8,128)(2,1)}, u32[]{:S(2)}, u32[]{:S(2)}) collective-permute-start(bf16[4,4,16,1792]{3,2,1,0:T(8,128)(2,1)} %collective-permute-done.16), channel_id=1, source_target_pairs={{0,16},{1,17},{2,18},{3,19},{4,20},{5,21},{6,22},{7,23},{8,56},{9,... | collective-permute-start | bytes 2752520 | tf_op jit(solution)/shard_map/ppermute | solution.py:58
  160.5 2.6 collective-permute-done.26
  167.3 3.3 %pad_maximum_fusion.5 = bf16[4,4,4,16,1664]{4,3,2,1,0:T(8,128)(2,1)} fusion(bf16[1,4,4,16,1664]{4,3,2,1,0:T(8,128)(2,1)} %bitcast.28, bf16[1,4,4,16,1664]{4,3,2,1,0:T(8,128)(2,1)} %bitcast.27, bf16[1,4,4,16,1664]{4,3,2,1,0:T(8,128)(2,1)} %bitcast.26, bf16[1,4,4,16,1664]{4,3,2,1,0:T(8,128)(2,1)S(1)} %get-tuple-element.10), kind=kLoop, calls=%fused_computation.15 | loop fusion | flops 5111808 | bytes 6815744 | tf_op jit(solution)/shard_map/stack | solution.py:59
  171.0 3.4 %pad_maximum_fusion.4 = bf16[4,4,4,16,1792]{4,3,0,2,1:T(8,128)(2,1)} fusion(bf16[1,4,4,16,1792]{4,3,0,2,1:T(8,128)(2,1)} %bitcast.44, bf16[1,4,4,16,1792]{4,3,0,2,1:T(8,128)(2,1)} %bitcast.43, bf16[1,4,4,16,1792]{4,3,0,2,1:T(8,128)(2,1)} %bitcast.41, bf16[1,4,4,16,1792]{4,3,0,2,1:T(8,128)(2,1)S(1)} %get-tuple-element.8), kind=kLoop, calls=%fused_computation.12 | loop fusion | flops 5505024 | bytes 7340032 | tf_op jit(solution)/shard_map/stack | solution.py:59
  174.4 12.8 %fusion.74 = (f32[1024]{0:T(1024)S(1)}, f32[1024,640]{0,1:T(8,128)}) fusion(bf16[5120,640]{1,0:T(8,128)(2,1)} %collective-permute-done.27, bf16[1024,1664]{1,0:T(8,128)(2,1)} %bitcast.132, bf16[1024,1792]{1,0:T(8,128)(2,1)} %bitcast.130, bf16[1024,1664]{1,0:T(8,128)(2,1)} %bitcast.134), kind=kOutput, calls=%fused_computation.158 | convolution fusion | flops 6742998016 | bytes 19664896 | tf_op jit(solution)/shard_map/dot_general | solution.py:170
  187.2 13.7 %collective-permute-start.28 = (f32[1024,640]{0,1:T(8,128)}, f32[1024,640]{0,1:T(8,128)}, u32[]{:S(2)}, u32[]{:S(2)}) collective-permute-start(f32[1024,640]{0,1:T(8,128)} %get-tuple-element.37), channel_id=1, source_target_pairs={{0,8},{1,9},{2,10},{3,11},{4,12},{5,13},{6,14},{7,15},{8,0},{9,1},... | collective-permute-start | bytes 7864328 | tf_op jit(solution)/shard_map/ppermute | solution.py:49
  200.9 12.8 %fusion.73 = (f32[1024]{0:T(1024)S(1)}, f32[1024,640]{0,1:T(8,128)}) fusion(bf16[5120,640]{1,0:T(8,128)(2,1)} %param.18, bf16[1024,1664]{1,0:T(8,128)(2,1)} %bitcast.133, bf16[1024,1792]{1,0:T(8,128)(2,1)} %bitcast.131, bf16[1024,1664]{1,0:T(8,128)(2,1)} %bitcast.135), kind=kOutput, calls=%fused_computation.157 | convolution fusion | flops 6742998016 | bytes 19664896 | tf_op jit(solution)/shard_map/dot_general | solution.py:169
  213.7 3.3 %fusion.1 = f32[1024]{0:T(1024)S(1)} fusion(f32[1024,640]{0,1:T(8,128)} %get-tuple-element.37, f32[1024,640]{0,1:T(8,128)} %get-tuple-element.35, f32[1024]{0:T(1024)S(1)} %reduce_max.63), kind=kLoop, calls=%fused_computation.6 | loop fusion | flops 3931136 | bytes 5251072 | tf_op jit(solution)/shard_map/reduce_sum | solution.py:80
  218.6 3.9 %all-to-all-start.3 = ((f32[16,1,1024]{2,1,0:T(1,128)}), f32[16,1,1024]{2,1,0:T(1,128)S(1)}, u32[]{:S(2)}, u32[]{:S(2)}) async-start(f32[16,1,1024]{2,1,0:T(1,128)} %reshape.501), calls=%async_computation.3 | async-start | bytes 131072 | tf_op jit(solution)/shard_map/all_to_all | solution.py:85
  222.7 5.6 %all-to-all-done.3 = f32[16,1,1024]{2,1,0:T(1,128)S(1)} async-done(((f32[16,1,1024]{2,1,0:T(1,128)}), f32[16,1,1024]{2,1,0:T(1,128)S(1)}, u32[]{:S(2)}, u32[]{:S(2)}) %all-to-all-start.3) | async-done | bytes 65568 | tf_op jit(solution)/shard_map/all_to_all | solution.py:85
  230.5 3.6 %all-to-all-start.4 = ((f32[8,1,2048]{2,1,0:T(1,128)}), f32[8,1,2048]{2,1,0:T(1,128)S(1)}, u32[]{:S(2)}, u32[]{:S(2)}) async-start(f32[8,1,2048]{2,1,0:T(1,128)} %reshape.503), calls=%async_computation.4 | async-start | bytes 131072 | tf_op jit(solution)/shard_map/all_to_all | solution.py:85
  234.2 6.5 %all-to-all-done.4 = f32[8,1,2048]{2,1,0:T(1,128)S(1)} async-done(((f32[8,1,2048]{2,1,0:T(1,128)}), f32[8,1,2048]{2,1,0:T(1,128)S(1)}, u32[]{:S(2)}, u32[]{:S(2)}) %all-to-all-start.4) | async-done | bytes 65568 | tf_op jit(solution)/shard_map/all_to_all | solution.py:85
  241.9 5.5 %pad_maximum_fusion.1 = f32[2048,640]{0,1:T(8,128)} fusion(f32[1024,640]{0,1:T(8,128)} %collective-permute-done.28, f32[1024,640]{0,1:T(8,128)} %get-tuple-element.35), kind=kLoop, calls=%fused_computation.3 | loop fusion | flops 1310720 | bytes 10485760 | tf_op jit(solution)/shard_map/concatenate | solution.py:199
  247.5 5.9 %copy.97 = f32[2048,640]{1,0:T(8,128)} copy(f32[2048,640]{0,1:T(8,128)} %pad_maximum_fusion.1) | data formatting | bytes 10485760 | tf_op jit(solution)/shard_map/concatenate | solution.py:199
  253.4 5.7 %gather_fusion = f32[128,16,640]{2,1,0:T(8,128)} fusion(f32[128,16,640]{2,1,0:T(8,128)} %bitcast.128, s32[1024]{0:T(1024)S(1)} %pad_clamp_fusion.1), kind=kCustom, calls=%fused_computation | custom fusion | bytes 10486272 | tf_op jit(solution)/shard_map/jit(_take)/gather | solution.py:200
  259.1 7.2 %gather.11 = f32[512,4,640]{2,1,0:T(4,128)} reshape(f32[128,16,640]{2,1,0:T(8,128)} %gather_fusion) | data formatting | bytes 10485760 | tf_op jit(solution)/shard_map/jit(_take)/gather | solution.py:200
  266.3 7.1 %select_subtract_fusion = f32[512,4,640]{2,1,0:T(4,128)} fusion(f32[512,4,640]{2,1,0:T(4,128)} %gather.11, f32[512,4]{1,0:T(8,128)S(1)} %sub.218, pred[512]{0:T(512)(128)(4,1)S(1)} %broadcast_in_dim.38), kind=kLoop, calls=%fused_computation.7 | loop fusion | flops 2621440 | bytes 10494464 | tf_op jit(solution)/shard_map/sub | solution.py:200
  (154 shorter events, 65.0 us)
Async XLA Ops:
  9.9 13.8 %all-to-all-start = ((bf16[16,8,768]{2,1,0:T(8,128)(2,1)}), bf16[16,8,768]{2,1,0:T(8,128)(2,1)S(1)}, u32[]{:S(2)}, u32[]{:S(2)}) async-start(bf16[16,8,768]{2,1,0:T(8,128)(2,1)} %fusion.16), calls=%async_computation | async-start | bytes 393216 | tf_op jit(solution)/shard_map/all_to_all | solution.py:127
  47.0 45.3 %all-to-all-start.2 = ((f32[8,16,5120]{2,1,0:T(8,128)}), f32[8,16,5120]{2,1,0:T(8,128)}, u32[]{:S(2)}, u32[]{:S(2)}) async-start(f32[8,16,5120]{2,1,0:T(8,128)} %bitcast.129), calls=%async_computation.2 | async-start | bytes 5242880 | tf_op jit(solution)/shard_map/all_to_all | solution.py:157
  54.3 120.0 %collective-permute-start.27 = (bf16[5120,640]{1,0:T(8,128)(2,1)}, bf16[5120,640]{1,0:T(8,128)(2,1)}, u32[]{:S(2)}, u32[]{:S(2)}) collective-permute-start(bf16[5120,640]{1,0:T(8,128)(2,1)} %param.18), channel_id=1, source_target_pairs={{0,8},{1,9},{2,10},{3,11},{4,12},{5,13},{6,14},{7,15},{8,0},{9,1},... | collective-permute-start | bytes 19660808 | tf_op jit(solution)/shard_map/ppermute | solution.py:49
  94.5 3.2 %collective-permute-start.18 = (bf16[16,1664]{1,0:T(8,128)(2,1)S(1)}, bf16[16,1664]{1,0:T(8,128)(2,1)S(1)}, u32[]{:S(2)}, u32[]{:S(2)}) collective-permute-start(bf16[16,1664]{1,0:T(8,128)(2,1)S(1)} %get-tuple-element.24), channel_id=1, source_target_pairs={{0,64},{1,65},{2,66},{3,67},{4,68},{5,69},{6,70},{7,71},{8,73},{9,... | collective-permute-start | bytes 159752 | tf_op jit(solution)/shard_map/ppermute | solution.py:58
  96.1 4.2 %collective-permute-start.9 = (bf16[16,1792]{1,0:T(8,128)(2,1)S(1)}, bf16[16,1792]{1,0:T(8,128)(2,1)S(1)}, u32[]{:S(2)}, u32[]{:S(2)}) collective-permute-start(bf16[16,1792]{1,0:T(8,128)(2,1)S(1)} %get-tuple-element.27), channel_id=1, source_target_pairs={{0,2},{1,3},{2,4},{3,5},{4,6},{5,7},{6,0},{7,1},{8,14},{9,15},{10,... | collective-permute-start | bytes 172040 | tf_op jit(solution)/shard_map/ppermute | solution.py:58
  96.9 4.3 %collective-permute-start = (bf16[16,1664]{1,0:T(8,128)(2,1)S(1)}, bf16[16,1664]{1,0:T(8,128)(2,1)S(1)}, u32[]{:S(2)}, u32[]{:S(2)}) collective-permute-start(bf16[16,1664]{1,0:T(8,128)(2,1)S(1)} %get-tuple-element.25), channel_id=1, source_target_pairs={{0,16},{1,17},{2,18},{3,19},{4,20},{5,21},{6,22},{7,23},{8,56},{9,... | collective-permute-start | bytes 159752 | tf_op jit(solution)/shard_map/ppermute | solution.py:58
  97.7 4.5 %collective-permute-start.19 = (bf16[16,1664]{1,0:T(8,128)(2,1)S(1)}, bf16[16,1664]{1,0:T(8,128)(2,1)S(1)}, u32[]{:S(2)}, u32[]{:S(2)}) collective-permute-start(bf16[16,1664]{1,0:T(8,128)(2,1)S(1)} %collective-permute-done.18), channel_id=1, source_target_pairs={{0,64},{1,65},{2,66},{3,67},{4,68},{5,69},{6,70},{7,71},{8,73},{9,... | collective-permute-start | bytes 159752 | tf_op jit(solution)/shard_map/ppermute | solution.py:58
  100.3 6.1 %collective-permute-start.10 = (bf16[16,1792]{1,0:T(8,128)(2,1)S(1)}, bf16[16,1792]{1,0:T(8,128)(2,1)S(1)}, u32[]{:S(2)}, u32[]{:S(2)}) collective-permute-start(bf16[16,1792]{1,0:T(8,128)(2,1)S(1)} %collective-permute-done.9), channel_id=1, source_target_pairs={{0,2},{1,3},{2,4},{3,5},{4,6},{5,7},{6,0},{7,1},{8,14},{9,15},{10,... | collective-permute-start | bytes 172040 | tf_op jit(solution)/shard_map/ppermute | solution.py:58
  101.2 3.3 %collective-permute-start.1 = (bf16[16,1664]{1,0:T(8,128)(2,1)S(1)}, bf16[16,1664]{1,0:T(8,128)(2,1)S(1)}, u32[]{:S(2)}, u32[]{:S(2)}) collective-permute-start(bf16[16,1664]{1,0:T(8,128)(2,1)S(1)} %collective-permute-done), channel_id=1, source_target_pairs={{0,16},{1,17},{2,18},{3,19},{4,20},{5,21},{6,22},{7,23},{8,56},{9,... | collective-permute-start | bytes 159752 | tf_op jit(solution)/shard_map/ppermute | solution.py:58
  102.3 4.2 %collective-permute-start.20 = (bf16[16,1664]{1,0:T(8,128)(2,1)S(1)}, bf16[16,1664]{1,0:T(8,128)(2,1)S(1)}, u32[]{:S(2)}, u32[]{:S(2)}) collective-permute-start(bf16[16,1664]{1,0:T(8,128)(2,1)S(1)} %collective-permute-done.19), channel_id=1, source_target_pairs={{0,64},{1,65},{2,66},{3,67},{4,68},{5,69},{6,70},{7,71},{8,73},{9,... | collective-permute-start | bytes 159752 | tf_op jit(solution)/shard_map/ppermute | solution.py:58
  104.5 6.0 %collective-permute-start.2 = (bf16[16,1664]{1,0:T(8,128)(2,1)S(1)}, bf16[16,1664]{1,0:T(8,128)(2,1)S(1)}, u32[]{:S(2)}, u32[]{:S(2)}) collective-permute-start(bf16[16,1664]{1,0:T(8,128)(2,1)S(1)} %collective-permute-done.1), channel_id=1, source_target_pairs={{0,16},{1,17},{2,18},{3,19},{4,20},{5,21},{6,22},{7,23},{8,56},{9,... | collective-permute-start | bytes 159752 | tf_op jit(solution)/shard_map/ppermute | solution.py:58
  106.5 5.7 %collective-permute-start.21 = (bf16[4,16,1664]{2,1,0:T(8,128)(2,1)S(1)}, bf16[4,16,1664]{2,1,0:T(8,128)(2,1)S(1)}, u32[]{:S(2)}, u32[]{:S(2)}) collective-permute-start(bf16[4,16,1664]{2,1,0:T(8,128)(2,1)S(1)} %get-tuple-element.19), channel_id=1, source_target_pairs={{0,16},{1,17},{2,18},{3,19},{4,20},{5,21},{6,22},{7,23},{8,56},{9,... | collective-permute-start | bytes 638984 | tf_op jit(solution)/shard_map/ppermute | solution.py:58
  109.5 4.9 %collective-permute-start.12 = (bf16[4,16,1792]{2,1,0:T(8,128)(2,1)S(1)}, bf16[4,16,1792]{2,1,0:T(8,128)(2,1)S(1)}, u32[]{:S(2)}, u32[]{:S(2)}) collective-permute-start(bf16[4,16,1792]{2,1,0:T(8,128)(2,1)S(1)} %get-tuple-element.15), channel_id=1, source_target_pairs={{0,64},{1,65},{2,66},{3,67},{4,68},{5,69},{6,70},{7,71},{8,73},{9,... | collective-permute-start | bytes 688136 | tf_op jit(solution)/shard_map/ppermute | solution.py:58
  110.6 6.3 %collective-permute-start.3 = (bf16[4,16,1664]{2,1,0:T(8,128)(2,1)S(1)}, bf16[4,16,1664]{2,1,0:T(8,128)(2,1)S(1)}, u32[]{:S(2)}, u32[]{:S(2)}) collective-permute-start(bf16[4,16,1664]{2,1,0:T(8,128)(2,1)S(1)} %get-tuple-element.17), channel_id=1, source_target_pairs={{0,2},{1,3},{2,4},{3,5},{4,6},{5,7},{6,0},{7,1},{8,14},{9,15},{10,... | collective-permute-start | bytes 638984 | tf_op jit(solution)/shard_map/ppermute | solution.py:58
  112.2 6.3 %collective-permute-start.22 = (bf16[4,16,1664]{2,1,0:T(8,128)(2,1)S(1)}, bf16[4,16,1664]{2,1,0:T(8,128)(2,1)S(1)}, u32[]{:S(2)}, u32[]{:S(2)}) collective-permute-start(bf16[4,16,1664]{2,1,0:T(8,128)(2,1)S(1)} %collective-permute-done.21), channel_id=1, source_target_pairs={{0,16},{1,17},{2,18},{3,19},{4,20},{5,21},{6,22},{7,23},{8,56},{9,... | collective-permute-start | bytes 638984 | tf_op jit(solution)/shard_map/ppermute | solution.py:58
  114.5 10.2 %collective-permute-start.13 = (bf16[4,16,1792]{2,1,0:T(8,128)(2,1)S(1)}, bf16[4,16,1792]{2,1,0:T(8,128)(2,1)S(1)}, u32[]{:S(2)}, u32[]{:S(2)}) collective-permute-start(bf16[4,16,1792]{2,1,0:T(8,128)(2,1)S(1)} %collective-permute-done.12), channel_id=1, source_target_pairs={{0,64},{1,65},{2,66},{3,67},{4,68},{5,69},{6,70},{7,71},{8,73},{9,... | collective-permute-start | bytes 688136 | tf_op jit(solution)/shard_map/ppermute | solution.py:58
  116.9 4.7 %collective-permute-start.4 = (bf16[4,16,1664]{2,1,0:T(8,128)(2,1)S(1)}, bf16[4,16,1664]{2,1,0:T(8,128)(2,1)S(1)}, u32[]{:S(2)}, u32[]{:S(2)}) collective-permute-start(bf16[4,16,1664]{2,1,0:T(8,128)(2,1)S(1)} %collective-permute-done.3), channel_id=1, source_target_pairs={{0,2},{1,3},{2,4},{3,5},{4,6},{5,7},{6,0},{7,1},{8,14},{9,15},{10,... | collective-permute-start | bytes 638984 | tf_op jit(solution)/shard_map/ppermute | solution.py:58
  118.5 6.2 %collective-permute-start.23 = (bf16[4,16,1664]{2,1,0:T(8,128)(2,1)S(1)}, bf16[4,16,1664]{2,1,0:T(8,128)(2,1)S(1)}, u32[]{:S(2)}, u32[]{:S(2)}) collective-permute-start(bf16[4,16,1664]{2,1,0:T(8,128)(2,1)S(1)} %collective-permute-done.22), channel_id=1, source_target_pairs={{0,16},{1,17},{2,18},{3,19},{4,20},{5,21},{6,22},{7,23},{8,56},{9,... | collective-permute-start | bytes 638984 | tf_op jit(solution)/shard_map/ppermute | solution.py:58
  121.6 5.8 %collective-permute-start.5 = (bf16[4,16,1664]{2,1,0:T(8,128)(2,1)S(1)}, bf16[4,16,1664]{2,1,0:T(8,128)(2,1)S(1)}, u32[]{:S(2)}, u32[]{:S(2)}) collective-permute-start(bf16[4,16,1664]{2,1,0:T(8,128)(2,1)S(1)} %collective-permute-done.4), channel_id=1, source_target_pairs={{0,2},{1,3},{2,4},{3,5},{4,6},{5,7},{6,0},{7,1},{8,14},{9,15},{10,... | collective-permute-start | bytes 638984 | tf_op jit(solution)/shard_map/ppermute | solution.py:58
  124.7 4.9 %collective-permute-start.14 = (bf16[4,16,1792]{2,1,0:T(8,128)(2,1)S(1)}, bf16[4,16,1792]{2,1,0:T(8,128)(2,1)S(1)}, u32[]{:S(2)}, u32[]{:S(2)}) collective-permute-start(bf16[4,16,1792]{2,1,0:T(8,128)(2,1)S(1)} %collective-permute-done.13), channel_id=1, source_target_pairs={{0,64},{1,65},{2,66},{3,67},{4,68},{5,69},{6,70},{7,71},{8,73},{9,... | collective-permute-start | bytes 688136 | tf_op jit(solution)/shard_map/ppermute | solution.py:58
  125.7 11.9 %collective-permute-start.24 = (bf16[4,4,16,1664]{3,2,1,0:T(8,128)(2,1)}, bf16[4,4,16,1664]{3,2,1,0:T(8,128)(2,1)}, u32[]{:S(2)}, u32[]{:S(2)}) collective-permute-start(bf16[4,4,16,1664]{3,2,1,0:T(8,128)(2,1)} %get-tuple-element.13), channel_id=1, source_target_pairs={{0,2},{1,3},{2,4},{3,5},{4,6},{5,7},{6,0},{7,1},{8,14},{9,15},{10,... | collective-permute-start | bytes 2555912 | tf_op jit(solution)/shard_map/ppermute | solution.py:58
  129.5 12.2 %collective-permute-start.6 = (bf16[4,4,16,1664]{3,2,1,0:T(8,128)(2,1)}, bf16[4,4,16,1664]{3,2,1,0:T(8,128)(2,1)}, u32[]{:S(2)}, u32[]{:S(2)}) collective-permute-start(bf16[4,4,16,1664]{3,2,1,0:T(8,128)(2,1)} %get-tuple-element.11), channel_id=1, source_target_pairs={{0,64},{1,65},{2,66},{3,67},{4,68},{5,69},{6,70},{7,71},{8,73},{9,... | collective-permute-start | bytes 2555912 | tf_op jit(solution)/shard_map/ppermute | solution.py:58
  130.6 12.9 %collective-permute-start.15 = (bf16[4,4,16,1792]{3,2,1,0:T(8,128)(2,1)}, bf16[4,4,16,1792]{3,2,1,0:T(8,128)(2,1)}, u32[]{:S(2)}, u32[]{:S(2)}) collective-permute-start(bf16[4,4,16,1792]{3,2,1,0:T(8,128)(2,1)} %get-tuple-element.9), channel_id=1, source_target_pairs={{0,16},{1,17},{2,18},{3,19},{4,20},{5,21},{6,22},{7,23},{8,56},{9,... | collective-permute-start | bytes 2752520 | tf_op jit(solution)/shard_map/ppermute | solution.py:58
  137.6 12.2 %collective-permute-start.25 = (bf16[4,4,16,1664]{3,2,1,0:T(8,128)(2,1)}, bf16[4,4,16,1664]{3,2,1,0:T(8,128)(2,1)}, u32[]{:S(2)}, u32[]{:S(2)}) collective-permute-start(bf16[4,4,16,1664]{3,2,1,0:T(8,128)(2,1)} %collective-permute-done.24), channel_id=1, source_target_pairs={{0,2},{1,3},{2,4},{3,5},{4,6},{5,7},{6,0},{7,1},{8,14},{9,15},{10,... | collective-permute-start | bytes 2555912 | tf_op jit(solution)/shard_map/ppermute | solution.py:58
  141.6 12.2 %collective-permute-start.7 = (bf16[4,4,16,1664]{3,2,1,0:T(8,128)(2,1)}, bf16[4,4,16,1664]{3,2,1,0:T(8,128)(2,1)}, u32[]{:S(2)}, u32[]{:S(2)}) collective-permute-start(bf16[4,4,16,1664]{3,2,1,0:T(8,128)(2,1)} %collective-permute-done.6), channel_id=1, source_target_pairs={{0,64},{1,65},{2,66},{3,67},{4,68},{5,69},{6,70},{7,71},{8,73},{9,... | collective-permute-start | bytes 2555912 | tf_op jit(solution)/shard_map/ppermute | solution.py:58
  143.5 13.5 %collective-permute-start.16 = (bf16[4,4,16,1792]{3,2,1,0:T(8,128)(2,1)}, bf16[4,4,16,1792]{3,2,1,0:T(8,128)(2,1)}, u32[]{:S(2)}, u32[]{:S(2)}) collective-permute-start(bf16[4,4,16,1792]{3,2,1,0:T(8,128)(2,1)} %collective-permute-done.15), channel_id=1, source_target_pairs={{0,16},{1,17},{2,18},{3,19},{4,20},{5,21},{6,22},{7,23},{8,56},{9,... | collective-permute-start | bytes 2752520 | tf_op jit(solution)/shard_map/ppermute | solution.py:58
  149.8 13.4 %collective-permute-start.26 = (bf16[4,4,16,1664]{3,2,1,0:T(8,128)(2,1)}, bf16[4,4,16,1664]{3,2,1,0:T(8,128)(2,1)}, u32[]{:S(2)}, u32[]{:S(2)}) collective-permute-start(bf16[4,4,16,1664]{3,2,1,0:T(8,128)(2,1)} %collective-permute-done.25), channel_id=1, source_target_pairs={{0,2},{1,3},{2,4},{3,5},{4,6},{5,7},{6,0},{7,1},{8,14},{9,15},{10,... | collective-permute-start | bytes 2555912 | tf_op jit(solution)/shard_map/ppermute | solution.py:58
  153.8 13.5 %collective-permute-start.8 = (bf16[4,4,16,1664]{3,2,1,0:T(8,128)(2,1)}, bf16[4,4,16,1664]{3,2,1,0:T(8,128)(2,1)}, u32[]{:S(2)}, u32[]{:S(2)}) collective-permute-start(bf16[4,4,16,1664]{3,2,1,0:T(8,128)(2,1)} %collective-permute-done.7), channel_id=1, source_target_pairs={{0,64},{1,65},{2,66},{3,67},{4,68},{5,69},{6,70},{7,71},{8,73},{9,... | collective-permute-start | bytes 2555912 | tf_op jit(solution)/shard_map/ppermute | solution.py:58
  156.9 14.1 %collective-permute-start.17 = (bf16[4,4,16,1792]{3,2,1,0:T(8,128)(2,1)}, bf16[4,4,16,1792]{3,2,1,0:T(8,128)(2,1)}, u32[]{:S(2)}, u32[]{:S(2)}) collective-permute-start(bf16[4,4,16,1792]{3,2,1,0:T(8,128)(2,1)} %collective-permute-done.16), channel_id=1, source_target_pairs={{0,16},{1,17},{2,18},{3,19},{4,20},{5,21},{6,22},{7,23},{8,56},{9,... | collective-permute-start | bytes 2752520 | tf_op jit(solution)/shard_map/ppermute | solution.py:58
  187.2 54.8 %collective-permute-start.28 = (f32[1024,640]{0,1:T(8,128)}, f32[1024,640]{0,1:T(8,128)}, u32[]{:S(2)}, u32[]{:S(2)}) collective-permute-start(f32[1024,640]{0,1:T(8,128)} %get-tuple-element.37), channel_id=1, source_target_pairs={{0,8},{1,9},{2,10},{3,11},{4,12},{5,13},{6,14},{7,15},{8,0},{9,1},... | collective-permute-start | bytes 7864328 | tf_op jit(solution)/shard_map/ppermute | solution.py:49
  218.6 9.7 %all-to-all-start.3 = ((f32[16,1,1024]{2,1,0:T(1,128)}), f32[16,1,1024]{2,1,0:T(1,128)S(1)}, u32[]{:S(2)}, u32[]{:S(2)}) async-start(f32[16,1,1024]{2,1,0:T(1,128)} %reshape.501), calls=%async_computation.3 | async-start | bytes 131072 | tf_op jit(solution)/shard_map/all_to_all | solution.py:85
  230.5 10.1 %all-to-all-start.4 = ((f32[8,1,2048]{2,1,0:T(1,128)}), f32[8,1,2048]{2,1,0:T(1,128)S(1)}, u32[]{:S(2)}, u32[]{:S(2)}) async-start(f32[8,1,2048]{2,1,0:T(1,128)} %reshape.503), calls=%async_computation.4 | async-start | bytes 131072 | tf_op jit(solution)/shard_map/all_to_all | solution.py:85
  (11 other events, 113.5 us)

commit v2 on v1

--- a/solution.py
+++ b/solution.py
@@ -1,12 +1,13 @@
 import jax
 import jax.numpy as jnp
-import numpy as np
 from jax import lax
+from jax.experimental import pallas as pl
+from jax.experimental.pallas import tpu as pltpu
 from jax.sharding import PartitionSpec as P
 
 BOTH = ("grp", "vocab")
 RING = 4
-PIECES = ((0, 1664), (1664, 3456), (3456, 5120))
+PIECES = ((0, 1792), (1792, 3584), (3584, 5120))
 ORDERS = ("xyz", "yzx", "zxy")
 
 
@@ -32,21 +33,22 @@
     return pairs
 
 
-def core_pairs():
+def swap_pairs(axis, distance, size):
     pairs = []
     for source in range(128):
         at = place_of(source)
-        at["core"] = 1 - at["core"]
+        at[axis] = (at[axis] + distance) % size
         pairs.append((source, flat_of(at)))
     return pairs
 
 
 STEP = {axis: ring_pairs(axis) for axis in "xyz"}
-SWAP = core_pairs()
+CORES = swap_pairs("core", 1, 2)
+HALVES = swap_pairs("z", 2, RING)
 
 
 def swap_cores(block):
-    return lax.ppermute(block, BOTH, SWAP)
+    return lax.ppermute(block, BOTH, CORES)
 
 
 def ring_gather(blocks):
@@ -56,8 +58,137 @@
         for _ in range(RING - 1):
             for k, order in enumerate(ORDERS):
                 rounds[k].append(lax.ppermute(rounds[k][-1], BOTH, STEP[order[stage]]))
-        held = [jnp.stack(parts) for parts in rounds]
-    return held
+        if stage < 2:
+            held = [jnp.stack(parts) for parts in rounds]
+    return rounds
+
+
+def head_kernel(*refs):
+    parts = (refs[0:4], refs[4:8], refs[8:12])
+    own_w, other_w, own_out, other_out, sums, *work = refs[12:]
+    lhs, weights, (total, lhs_sem, w_sem, out_sem) = work[0:3], work[3:6], work[6:]
+    half = own_w.shape[1]
+
+    def weight_copies(k):
+        a, b = PIECES[k]
+        rows = pl.ds(a, b - a)
+        return [
+            pltpu.make_async_copy(own_w.at[rows], weights[k].at[:, pl.ds(0, half)], w_sem.at[k, 0]),
+            pltpu.make_async_copy(
+                other_w.at[rows], weights[k].at[:, pl.ds(half, half)], w_sem.at[k, 1]
+            ),
+        ]
+
+    def part_copies(k):
+        return [
+            pltpu.make_async_copy(parts[k][r], lhs[k].at[r], lhs_sem.at[k, r]) for r in range(RING)
+        ]
+
+    def out_copies(z):
+        rows = pl.ds(z * 256, 256)
+        return [
+            pltpu.make_async_copy(total.at[rows, pl.ds(0, half)], own_out.at[rows], out_sem.at[z, 0]),
+            pltpu.make_async_copy(
+                total.at[rows, pl.ds(half, half)], other_out.at[rows], out_sem.at[z, 1]
+            ),
+        ]
+
+    for k in range(3):
+        for copy in part_copies(k) + weight_copies(k):
+            copy.start()
+
+    def rows_of(k, z):
+        if k == 0:
+            blocks = [lhs[0][z, y, x] for y in range(4) for x in range(4)]
+        elif k == 1:
+            blocks = [lhs[1][x, z, y] for y in range(4) for x in range(4)]
+        else:
+            blocks = [lhs[2][y, x, z] for y in range(4) for x in range(4)]
+        return jnp.concatenate(blocks, axis=0)
+
+    for k in range(3):
+        for copy in part_copies(k) + weight_copies(k):
+            copy.wait()
+
+        def tile(z, carry, k=k):
+            rows = pl.ds(pl.multiple_of(z * 256, 256), 256)
+            fresh = jnp.dot(rows_of(k, z), weights[k][...], preferred_element_type=jnp.float32)
+            if k > 0:
+                fresh = total[rows] + fresh
+            total[rows] = fresh
+            if k == 2:
+                for copy in out_copies(z):
+                    copy.start()
+                top = jnp.max(fresh, axis=1, keepdims=True)
+                sums[rows] = top + jnp.log(jnp.sum(jnp.exp(fresh - top), axis=1, keepdims=True))
+            return carry
+
+        lax.fori_loop(0, RING, tile, 0)
+    for z in range(RING):
+        for copy in out_copies(z):
+            copy.wait()
+
+
+def head_logits(rounds, own_w, other_w, mine):
+    half = own_w.shape[1]
+    rows = 64 * mine
+    anywhere = pl.BlockSpec(memory_space=pl.ANY)
+    widths = [b - a for a, b in PIECES]
+    return pl.pallas_call(
+        head_kernel,
+        out_shape=(
+            jax.ShapeDtypeStruct((rows, half), jnp.float32),
+            jax.ShapeDtypeStruct((rows, half), jnp.float32),
+            jax.ShapeDtypeStruct((rows, 1), jnp.float32),
+        ),
+        in_specs=[anywhere] * 14,
+        out_specs=(anywhere, anywhere, pl.BlockSpec(memory_space=pltpu.VMEM)),
+        scratch_shapes=[pltpu.VMEM((4, 4, 4, mine, w), jnp.bfloat16) for w in widths]
+        + [pltpu.VMEM((w, 2 * half), jnp.bfloat16) for w in widths]
+        + [
+            pltpu.VMEM((rows, 2 * half), jnp.float32),
+            pltpu.SemaphoreType.DMA((3, RING)),
+            pltpu.SemaphoreType.DMA((3, 2)),
+            pltpu.SemaphoreType.DMA((RING, 2)),
+        ],
+        compiler_params=pltpu.CompilerParams(vmem_limit_bytes=52 * 2**20),
+        name="head",
+    )(*rounds[0], *rounds[1], *rounds[2], own_w, other_w)
+
+
+def output_kernel(order, place, own, other, totals, out):
+    pair = pl.program_id(0)
+    y, z_hi = pair // 2, pair % 2
+    core, x_here, y_here, z_here = place[0], place[1], place[2], place[3]
+    for ref, plane in ((own, core), (other, 1 - core)):
+        sign = 1 - 2 * plane
+        away = lambda here, there: (sign * (here - there)) & 3
+        for z_lo in range(2):
+            for x in range(4):
+                prompt = z_lo * 8 + x * 2 + plane
+                block = ref[away(z_here, z_hi * 2 + z_lo), away(y_here, y), away(x_here, x)]
+                block = block - totals[prompt, pair]
+                for row in range(4):
+                    near, which = divmod(row, 2)
+                    to = order[(pair * 2 + near) * 32 + prompt * 2 + which]
+                    out[near * 32 + to] = block[row * 4 : row * 4 + 4]
+
+
+def ordered_output(order, place, own, other, totals):
+    width = own.shape[-1]
+    whole = lambda a: pl.BlockSpec(a.shape, lambda i, *_: (0,) * a.ndim)
+    return pl.pallas_call(
+        output_kernel,
+        out_shape=jax.ShapeDtypeStruct((512, 4, width), jnp.float32),
+        grid_spec=pltpu.PrefetchScalarGridSpec(
+            num_scalar_prefetch=2,
+            grid=(8,),
+            in_specs=[whole(own), whole(other), whole(totals)],
+            out_specs=pl.BlockSpec((64, 4, width), lambda i, *_: (i, 0, 0)),
+        ),
+        compiler_params=pltpu.CompilerParams(vmem_limit_bytes=52 * 2**20),
+        name="output",
+    )(order, place, own, other, totals)
 
 
 def rms_scale(rows, gain):
@@ -106,6 +237,14 @@
     rows = samples * steps
     scale = 1.0 / head**0.5
     other_weight = swap_cores(head_weight)
+    core = lax.axis_index("grp") % 2
+    z_hi = lax.axis_index("vocab") % 2
+    z = z_hi * 2 + lax.axis_index("grp") // 8
+    y = lax.axis_index("vocab") // 2
+    x = (lax.axis_index("grp") // 2) % 4
+    shares = lax.axis_size("vocab")
+    span = width // shares
+    first_column = lax.axis_index("vocab") * span
 
     flat_rows = embedded.reshape(rows, width)
     normed_input = rms_scale(flat_rows.astype(jnp.float32), attn_gain).astype(jnp.bfloat16)
@@ -113,7 +252,13 @@
         jnp.bfloat16
     )
     projected = jnp.concatenate(
-        [project(query_weight), project(key_weight), project(value_weight)], axis=1
+        [
+            project(query_weight),
+            project(key_weight),
+            project(value_weight),
+            lax.dynamic_slice_in_dim(flat_rows, first_column, span, 1),
+        ],
+        axis=1,
     )
 
     same = sample_prompt[:, None] == sample_prompt[None, :]
@@ -129,7 +274,7 @@
     cut = groups * head
     queries = local[:, :cut].reshape(samples, steps, groups, head)
     new_keys = local[:, cut : cut + head].reshape(samples, steps, head)
-    new_values = local[:, cut + head :].reshape(samples, steps, head)
+    new_values = local[:, cut + head : cut + 2 * head].reshape(samples, steps, head)
     scores = (
         jnp.einsum("stgh,lh->stgl", queries, prefix_keys[0, 0], preferred_element_type=jnp.float32)
         * scale
@@ -149,56 +294,52 @@
     denominator = prefix_total * prefix_factor + new_total * new_factor
     attended = (numerator / denominator[..., None]).astype(jnp.bfloat16).reshape(rows, cut)
 
-    back = lax.all_to_all(attended, "grp", 0, 0, tiled=True)
-    attended = jnp.dot(to_sorted.T, back, preferred_element_type=jnp.float32).astype(jnp.bfloat16)
     partial_heads = jnp.dot(attended, out_weight, preferred_element_type=jnp.float32)
-    shares = lax.axis_size("vocab")
+    chunk = lax.dynamic_slice_in_dim(partial_heads, first_column, span, 1)
+    chunk = chunk + local[:, cut + 2 * head :].astype(jnp.float32)
+    partial_heads = lax.dynamic_update_slice_in_dim(partial_heads, chunk, first_column, 1)
     mine = rows // shares
-    arrived = lax.all_to_all(partial_heads, "vocab", 0, 0, tiled=True)
-    summed = jnp.sum(arrived.reshape(shares, mine, width), axis=0)
-    own_rows = lax.dynamic_slice_in_dim(flat_rows, lax.axis_index("vocab") * mine, mine, 0)
-    normed = rms_scale(own_rows.astype(jnp.float32) + summed, final_gain).astype(jnp.bfloat16)
-
-    gathered = ring_gather([normed[:, a:b] for a, b in PIECES])
-    turned = (
-        gathered[0],
-        gathered[1].transpose(1, 2, 0, 3, 4),
-        gathered[2].transpose(2, 0, 1, 3, 4),
-    )
-    plane = jnp.concatenate([t.reshape(64 * mine, t.shape[-1]) for t in turned], axis=1)
-    logits = jnp.dot(plane, head_weight, preferred_element_type=jnp.float32)
-    other_logits = jnp.dot(plane, other_weight, preferred_element_type=jnp.float32)
+    along_y = [[at * 2 + half for at in range(4)] for half in range(2)]
+    arrived = lax.all_to_all(
+        partial_heads, "vocab", 0, 0, tiled=True, axis_index_groups=along_y
+    ).reshape(4, 2, mine, width)
+    kept = jnp.sum(lax.dynamic_index_in_dim(arrived, z_hi, 1, False), axis=0)
+    given = jnp.sum(lax.dynamic_index_in_dim(arrived, 1 - z_hi, 1, False), axis=0)
+    hidden = kept + lax.ppermute(given, BOTH, HALVES)
+    normed = rms_scale(hidden, final_gain).astype(jnp.bfloat16)
+
+    rounds = ring_gather([normed[:, a:b] for a, b in PIECES])
+    logits, other_logits, local_sum = head_logits(rounds, head_weight, other_weight, mine)
     crossed = swap_cores(other_logits)
 
-    core = lax.axis_index("grp") % 2
-    z = (lax.axis_index("vocab") % 2) * 2 + lax.axis_index("grp") // 8
-    y = lax.axis_index("vocab") // 2
-    x = (lax.axis_index("grp") // 2) % 4
     places = jnp.arange(4, dtype=jnp.int32)
-    near = lambda c, at: jnp.where(c == 0, at - places, places - at) % 4
-    find = lambda c: (
-        near(c, z)[:, None, None] * 16 + near(c, y)[None, :, None] * 4 + near(c, x)[None, None, :]
-    )
-
-    local_sum = log_sum(jnp.concatenate([logits, other_logits], axis=1), 1)
-    mine_order = find(core).reshape(64)
+    near = lambda at: jnp.where(core == 0, at - places, places - at) % 4
+    mine_order = (
+        near(z)[:, None, None] * 16 + near(y)[None, :, None] * 4 + near(x)[None, None, :]
+    ).reshape(64)
     local_sum = jnp.take(local_sum.reshape(64, mine), mine_order, axis=0)
-    over_grp = spread(local_sum, "grp").reshape(8, 2, 64, mine)
-    over_grp = log_sum(over_grp, 0)
-    total = log_sum(spread(over_grp, "vocab").reshape(shares, 2, 64, mine), 0)
-
-    def rearrange(blocks):
-        return blocks.transpose((2, 4, 0, 3, 1) + tuple(range(5, blocks.ndim)))
-
-    total = rearrange(total.reshape(2, 2, 2, 4, 4, mine))
-    own_at = find(core).reshape(64)
-    other_at = find(1 - core).reshape(64) + 64
-    first = jnp.where(core == 0, own_at, other_at)
-    second = jnp.where(core == 0, other_at, own_at)
-    source = rearrange(jnp.stack([first, second]).reshape(2, 2, 2, 4, 4)).reshape(128)
-    blocks = jnp.concatenate([logits, crossed]).reshape(128, mine, head_weight.shape[1])
-    result = jnp.take(blocks, source, axis=0) - total.reshape(128, mine, 1)
-    return result.reshape(-1, steps, head_weight.shape[1])
+    sample_at = jnp.sum(
+        jnp.where(
+            slot[None, :] == jnp.arange(samples, dtype=jnp.int32)[:, None],
+            jnp.arange(samples, dtype=jnp.int32)[None, :],
+            0,
+        ),
+        axis=1,
+    )
+    sent = jnp.concatenate([local_sum.reshape(64 * mine), sample_at.astype(jnp.float32)])
+    over_grp = spread(sent, "grp")
+    order = over_grp[:, 64 * mine :].astype(jnp.int32).reshape(-1)
+    over_grp = log_sum(over_grp[:, : 64 * mine].reshape(8, 2, 64 * mine), 0)
+    total = log_sum(spread(over_grp, "vocab").reshape(shares, 2, 64 * mine), 0)
+    total = total.reshape(2, 2, 2, 4, 4, mine).transpose(2, 4, 0, 3, 1, 5)
+    shape = (4, 4, 4, mine, head_weight.shape[1])
+    return ordered_output(
+        order,
+        jnp.stack([core, x, y, z]).astype(jnp.int32),
+        logits.reshape(shape),
+        crossed.reshape(shape),
+        total.reshape(16, 8, mine, 1),
+    )
 
 
 def solution(mesh):

time: 275 us -> 239 us (0.87)
  other arithmetic: 39.1 us -> 8.05 us
  Pallas kernels: 0 us -> 28.7 us
  matrix products: 40.1 us -> 14.4 us
  waiting for transfers between devices: 79.8 us -> 99.1 us
  local copies, waits for them, and re-layouts: 28.6 us -> 12 us
  blocking collectives: 9.11 us -> 0 us
    pallas_call x0 -> x2, Pallas kernels: none -> 28.7 us  [the longest x1 21.4 us: head_logits(): pl.pallas_call(head_kernel, out_shape=(jax.ShapeDtypeStruct((rows, half),...]
    dot_general x2 -> x0, matrix products: 25.6 us -> none  [the longest x1 12.8 us: on_device(): jnp.dot(plane, other_weight, preferred_element_type=jnp.float32)]
    ppermute x27, waiting for transfers between devices: 23.8 us -> 44.1 us  [ring_gather(): rounds[k].append(lax.ppermute(rounds[k][-1], BOTH, STEP[order[stage]]))]
    gather x2 -> x0, local copies, waits for them, and re-layouts: 12.9 us -> none  [on_device(): result = jnp.take(blocks, source, axis=0) - total.reshape(128, mine, 1)]
    another operation x8 -> x6, other arithmetic: 11 us -> 0.45 us  [ring_gather(): held = [jnp.stack(parts) for parts in rounds]]
    all_to_all x1 -> x0, blocking collectives: 9.11 us -> none  [on_device(): back = lax.all_to_all(attended, 'grp', 0, 0, tiled=True)]
    sub x1 -> x0, other arithmetic: 7.15 us -> none  [on_device(): result = jnp.take(blocks, source, axis=0) - total.reshape(128, mine, 1)]
    all_to_all x1, waiting for transfers between devices: 37.2 us -> 31 us  [on_device(): lax.all_to_all(partial_heads, 'vocab', 0, 0, tiled=True, axis_index_group...]
  transfers between devices with their start and end apart: 33 -> 34, of which waited for: 17 -> 17; matrix products, arithmetic and copies ran while one was open for 14% -> 2% of each run, Pallas kernels for 0% -> 0%
where the time goes in v2:
time: 239 us; the launch traced here: 238 us
  waiting for transfers between devices  99.1 us (41%)
  starting transfers between devices  75.1 us (31%)
  Pallas kernels  28.7 us (12%)
  matrix products  14.4 us (6%)
  local copies, waits for them, and re-layouts  12 us (5%)
  other arithmetic  8.05 us (3%)
    ppermute x27, waiting for transfers between devices, ring_gather(): rounds[k].append(lax.ppermute(rounds[k][-1], BOTH, STEP[order[stage]]))  44.1 us
    ppermute x27, starting transfers between devices, ring_gather(): rounds[k].append(lax.ppermute(rounds[k][-1], BOTH, STEP[order[stage]]))  36.9 us
    all_to_all x1, waiting for transfers between devices, on_device(): lax.all_to_all(partial_heads, 'vocab', 0, 0, tiled=True, axis_index_group...  31 us
    pallas_call x1, Pallas kernels, head_logits(): pl.pallas_call(head_kernel, out_shape=(jax.ShapeDtypeStruct((rows, half),...  21.4 us
    ppermute x2, starting transfers between devices, swap_cores(): return lax.ppermute(block, BOTH, CORES)  13.9 us
    all_to_all x2, waiting for transfers between devices, spread(): lax.all_to_all(jnp.broadcast_to(values[None], (copies,) + values.shape),...  12.3 us
    all_to_all x2, starting transfers between devices, spread(): lax.all_to_all(jnp.broadcast_to(values[None], (copies,) + values.shape),...  9.25 us
    all_to_all x1, waiting for transfers between devices, on_device(): local = lax.all_to_all(sorted_rows, 'grp', 0, 0, tiled=True)  7.94 us
  transfers between devices with their start and end apart: 34, of which 17 were waited for; matrix products, arithmetic and copies ran while one was open for 2% of the time, Pallas kernels for 0%

profile of v2, /device:TPU:1, one launch (start us, length us, event | category | flops | bytes accessed | tf_op | source)
XLA Modules:
  0.0 237.9 jit_solution(17453384357895606401)
XLA Ops:
  0.0 3.5 %reshape.278 = bf16[128,5120]{1,0:T(8,128)(2,1)} reshape(bf16[32,4,5120]{2,1,0:T(4,128)(2,1)} %param.11) | data formatting | bytes 2621440 | tf_op jit(solution)/shard_map/reshape | solution.py:249
  5.6 2.1 convolution_convert_fusion.2
  10.0 3.4 %convolution_convert_fusion.1 = bf16[128,512]{1,0:T(8,128)(2,1)S(1)} fusion(bf16[5120,512]{1,0:T(8,128)(2,1)} %param.13, bf16[128,5120]{1,0:T(8,128)(2,1)S(1)} %copy-done.8, f32[5120]{0:T(1024)S(1)} %copy-done.16, f32[128]{0:T(128)S(1)} %rsqrt.20), kind=kOutput, calls=%fused_computation.16 | convolution fusion | flops 673775616 | bytes 6705664 | tf_op jit(solution)/shard_map/dot_general | solution.py:251
  14.6 7.2 %all-to-all-start = ((bf16[16,8,1408]{2,1,0:T(8,128)(2,1)}), bf16[16,8,1408]{2,1,0:T(8,128)(2,1)S(1)}, u32[]{:S(2)}, u32[]{:S(2)}) async-start(bf16[16,8,1408]{2,1,0:T(8,128)(2,1)} %fusion.2), calls=%async_computation | async-start | bytes 720896 | tf_op jit(solution)/shard_map/all_to_all | solution.py:272
  21.7 7.9 %all-to-all-done = bf16[16,8,1408]{2,1,0:T(8,128)(2,1)S(1)} async-done(((bf16[16,8,1408]{2,1,0:T(8,128)(2,1)}), bf16[16,8,1408]{2,1,0:T(8,128)(2,1)S(1)}, u32[]{:S(2)}, u32[]{:S(2)}) %all-to-all-start) | async-done | bytes 360480 | tf_op jit(solution)/shard_map/all_to_all | solution.py:272
  29.8 2.7 %multiply_reduce_fusion = (f32[32,4,4]{0,2,1:T(4,128)S(1)}, f32[32,4,4,2048]{3,0,2,1:T(8,128)}) fusion(bf16[1,1,2048,128]{3,2,1,0:T(8,128)(2,1)S(1)} %copy-done.12, bf16[32,4,4,128]{3,2,1,0:T(4,128)(2,1)S(1)} %reshape.279), kind=kOutput, calls=%fused_computation.2 | convolution fusion | flops 270532096 | bytes 4851712 | tf_op jit(solution)/shard_map/stgh,lh->stgl/dot_general | solution.py:279
  34.6 3.2 %fusion = f32[32,4,4]{0,2,1:T(4,128)S(1)} fusion(f32[32,4,4,2048]{3,0,2,1:T(8,128)} %get-tuple-element.37, f32[32,4,4]{0,2,1:T(4,128)S(1)} %get-tuple-element.36), kind=kLoop, calls=%fused_computation.3 | loop fusion | flops 3145216 | bytes 4198400 | tf_op jit(solution)/shard_map/reduce_sum | solution.py:202
  42.8 4.6 %all-to-all-start.1 = ((f32[4,32,5120]{2,1,0:T(8,128)}), f32[4,32,5120]{2,1,0:T(8,128)}, u32[]{:S(2)}, u32[]{:S(2)}) async-start(f32[4,32,5120]{2,1,0:T(8,128)} %bitcast.94), calls=%async_computation.1 | async-start | bytes 5242880 | tf_op jit(solution)/shard_map/all_to_all | solution.py:303
  47.4 31.0 %all-to-all-done.1 = f32[4,32,5120]{2,1,0:T(8,128)} async-done(((f32[4,32,5120]{2,1,0:T(8,128)}), f32[4,32,5120]{2,1,0:T(8,128)}, u32[]{:S(2)}, u32[]{:S(2)}) %all-to-all-start.1) | async-done | bytes 2621472 | tf_op jit(solution)/shard_map/all_to_all | solution.py:303
  80.3 3.4 %collective-permute-start = (f32[16,5120]{1,0:T(8,128)S(1)}, f32[16,5120]{1,0:T(8,128)S(1)}, u32[]{:S(2)}, u32[]{:S(2)}) collective-permute-start(f32[16,5120]{1,0:T(8,128)S(1)} %get-tuple-element.11), channel_id=1, source_target_pairs={{0,1},{1,0},{2,3},{3,2},{4,5},{5,4},{6,7},{7,6},{8,9},{9,8},{10,11... | collective-permute-start | bytes 983048 | tf_op jit(solution)/shard_map/ppermute | solution.py:308
  83.7 2.2 collective-permute-start.28
  85.9 3.9 %collective-permute-done = f32[16,5120]{1,0:T(8,128)S(1)} collective-permute-done((f32[16,5120]{1,0:T(8,128)S(1)}, f32[16,5120]{1,0:T(8,128)S(1)}, u32[]{:S(2)}, u32[]{:S(2)}) %collective-permute-start) | collective-permute-done | bytes 327712 | tf_op jit(solution)/shard_map/ppermute | solution.py:308
  90.1 4.0 %collective-permute-start.1 = (bf16[16,1792]{1,0:T(8,128)(2,1)S(1)}, bf16[16,1792]{1,0:T(8,128)(2,1)S(1)}, u32[]{:S(2)}, u32[]{:S(2)}) collective-permute-start(bf16[16,1792]{1,0:T(8,128)(2,1)S(1)} %get-tuple-element.33), channel_id=1, source_target_pairs={{0,16},{1,17},{2,18},{3,19},{4,20},{5,21},{6,22},{7,23},{8,56},{9,... | collective-permute-start | bytes 172040 | tf_op jit(solution)/shard_map/ppermute | solution.py:60
  95.4 3.0 %collective-permute-start.2 = (bf16[16,1792]{1,0:T(8,128)(2,1)S(1)}, bf16[16,1792]{1,0:T(8,128)(2,1)S(1)}, u32[]{:S(2)}, u32[]{:S(2)}) collective-permute-start(bf16[16,1792]{1,0:T(8,128)(2,1)S(1)} %collective-permute-done.1), channel_id=1, source_target_pairs={{0,16},{1,17},{2,18},{3,19},{4,20},{5,21},{6,22},{7,23},{8,56},{9,... | collective-permute-start | bytes 172040 | tf_op jit(solution)/shard_map/ppermute | solution.py:60
  100.2 2.4 %collective-permute-start.3 = (bf16[16,1792]{1,0:T(8,128)(2,1)S(1)}, bf16[16,1792]{1,0:T(8,128)(2,1)S(1)}, u32[]{:S(2)}, u32[]{:S(2)}) collective-permute-start(bf16[16,1792]{1,0:T(8,128)(2,1)S(1)} %collective-permute-done.2), channel_id=1, source_target_pairs={{0,16},{1,17},{2,18},{3,19},{4,20},{5,21},{6,22},{7,23},{8,56},{9,... | collective-permute-start | bytes 172040 | tf_op jit(solution)/shard_map/ppermute | solution.py:60
  105.6 2.4 %collective-permute-start.21 = (bf16[16,1536]{1,0:T(8,128)(2,1)S(1)}, bf16[16,1536]{1,0:T(8,128)(2,1)S(1)}, u32[]{:S(2)}, u32[]{:S(2)}) collective-permute-start(bf16[16,1536]{1,0:T(8,128)(2,1)S(1)} %collective-permute-done.20), channel_id=1, source_target_pairs={{0,64},{1,65},{2,66},{3,67},{4,68},{5,69},{6,70},{7,71},{8,73},{9,... | collective-permute-start | bytes 147464 | tf_op jit(solution)/shard_map/ppermute | solution.py:60
  108.7 2.3 collective-permute-done.12
  118.7 2.7 %collective-permute-start.6 = (bf16[4,16,1792]{2,1,0:T(8,128)(2,1)S(1)}, bf16[4,16,1792]{2,1,0:T(8,128)(2,1)S(1)}, u32[]{:S(2)}, u32[]{:S(2)}) collective-permute-start(bf16[4,16,1792]{2,1,0:T(8,128)(2,1)S(1)} %collective-permute-done.5), channel_id=1, source_target_pairs={{0,2},{1,3},{2,4},{3,5},{4,6},{5,7},{6,0},{7,1},{8,14},{9,15},{10,... | collective-permute-start | bytes 688136 | tf_op jit(solution)/shard_map/ppermute | solution.py:60
  121.4 4.5 %collective-permute-done.23 = bf16[4,16,1536]{2,1,0:T(8,128)(2,1)S(1)} collective-permute-done((bf16[4,16,1536]{2,1,0:T(8,128)(2,1)S(1)}, bf16[4,16,1536]{2,1,0:T(8,128)(2,1)S(1)}, u32[]{:S(2)}, u32[]{:S(2)}) %collective-permute-start.23) | collective-permute-done | bytes 196640 | tf_op jit(solution)/shard_map/ppermute | solution.py:60
  129.2 2.8 %collective-permute-done.15 = bf16[4,16,1792]{2,1,0:T(8,128)(2,1)S(1)} collective-permute-done((bf16[4,16,1792]{2,1,0:T(8,128)(2,1)S(1)}, bf16[4,16,1792]{2,1,0:T(8,128)(2,1)S(1)}, u32[]{:S(2)}, u32[]{:S(2)}) %collective-permute-start.15) | collective-permute-done | bytes 229408 | tf_op jit(solution)/shard_map/ppermute | solution.py:60
  133.0 9.2 %collective-permute-done.7.refs_1_ = bf16[4,4,16,1792]{3,2,1,0:T(8,128)(2,1)S(1)} collective-permute-done((bf16[4,4,16,1792]{3,2,1,0:T(8,128)(2,1)S(1)}, bf16[4,4,16,1792]{3,2,1,0:T(8,128)(2,1)S(1)}, u32[]{:S(2)}, u32[]{:S(2)}) %collective-permute-start.7) | collective-permute-done | bytes 917536 | tf_op jit(solution)/shard_map/ppermute | solution.py:60
  146.6 8.2 %collective-permute-done.8.refs_2_ = bf16[4,4,16,1792]{3,2,1,0:T(8,128)(2,1)} collective-permute-done((bf16[4,4,16,1792]{3,2,1,0:T(8,128)(2,1)S(1)}, bf16[4,4,16,1792]{3,2,1,0:T(8,128)(2,1)}, u32[]{:S(2)}, u32[]{:S(2)}) %collective-permute-start.8) | collective-permute-done | bytes 917536 | tf_op jit(solution)/shard_map/ppermute | solution.py:60
  154.8 2.9 %collective-permute-start.9 = (bf16[4,4,16,1792]{3,2,1,0:T(8,128)(2,1)}, bf16[4,4,16,1792]{3,2,1,0:T(8,128)(2,1)}, u32[]{:S(2)}, u32[]{:S(2)}) collective-permute-start(bf16[4,4,16,1792]{3,2,1,0:T(8,128)(2,1)} %collective-permute-done.8.refs_2_), channel_id=1, source_target_pairs={{0,64},{1,65},{2,66},{3,67},{4,68},{5,69},{6,70},{7,71},{8,73},{9,... | collective-permute-start | bytes 2752520 | tf_op jit(solution)/shard_map/ppermute | solution.py:60
  157.7 2.4 %collective-permute-start.18 = (bf16[4,4,16,1792]{3,2,1,0:T(8,128)(2,1)}, bf16[4,4,16,1792]{3,2,1,0:T(8,128)(2,1)}, u32[]{:S(2)}, u32[]{:S(2)}) collective-permute-start(bf16[4,4,16,1792]{3,2,1,0:T(8,128)(2,1)} %collective-permute-done.17.refs_6_), channel_id=1, source_target_pairs={{0,16},{1,17},{2,18},{3,19},{4,20},{5,21},{6,22},{7,23},{8,56},{9,... | collective-permute-start | bytes 2752520 | tf_op jit(solution)/shard_map/ppermute | solution.py:60
  160.4 11.2 %collective-permute-done.27.refs_11_ = bf16[4,4,16,1536]{3,2,1,0:T(8,128)(2,1)} collective-permute-done((bf16[4,4,16,1536]{3,2,1,0:T(8,128)(2,1)}, bf16[4,4,16,1536]{3,2,1,0:T(8,128)(2,1)}, u32[]{:S(2)}, u32[]{:S(2)}) %collective-permute-start.27) | collective-permute-done | bytes 786464 | tf_op jit(solution)/shard_map/ppermute | solution.py:60
  171.6 21.4 %head.1 = (f32[1024,640]{1,0:T(8,128)}, f32[1024,640]{1,0:T(8,128)}, f32[1024,1]{1,0:T(8,128)S(1)}) custom-call(bf16[4,4,16,1792]{3,2,1,0:T(8,128)(2,1)} %copy-done.6, bf16[4,4,16,1792]{3,2,1,0:T(8,128)(2,1)} %copy-done.9, bf16[4,4,16,1792]{3,2,1,0:T(8,128)(2,1)} %collective-permute-done.8.refs_2_, bf16[4,4,16,1792]{3,2,1,0:T(8,128)(2,1)} %collective-permute-done.9.refs_3_, ...), custom_call_target="tpu_custom_call" | custom-call | tf_op jit(solution)/shard_map/head/pallas_call | solution.py:137
  193.1 11.7 %collective-permute-start.29 = (f32[1024,640]{1,0:T(8,128)}, f32[1024,640]{1,0:T(8,128)}, u32[]{:S(2)}, u32[]{:S(2)}) collective-permute-start(f32[1024,640]{1,0:T(8,128)} %get-tuple-element.10), channel_id=1, source_target_pairs={{0,8},{1,9},{2,10},{3,11},{4,12},{5,13},{6,14},{7,15},{8,0},{9,1},... | collective-permute-start | bytes 7864328 | tf_op jit(solution)/shard_map/ppermute | solution.py:51
  207.0 3.4 %all-to-all-start.2 = ((f32[16,1,1056]{2,1,0:T(1,128)}), f32[16,1,1056]{2,1,0:T(1,128)S(1)}, u32[]{:S(2)}, u32[]{:S(2)}) async-start(f32[16,1,1056]{2,1,0:T(1,128)} %broadcast_in_dim.37), calls=%async_computation.2 | async-start | bytes 147456 | tf_op jit(solution)/shard_map/all_to_all | solution.py:216
  210.5 5.7 %all-to-all-done.2 = f32[16,1,1056]{2,1,0:T(1,128)S(1)} async-done(((f32[16,1,1056]{2,1,0:T(1,128)}), f32[16,1,1056]{2,1,0:T(1,128)S(1)}, u32[]{:S(2)}, u32[]{:S(2)}) %all-to-all-start.2) | async-done | bytes 67616 | tf_op jit(solution)/shard_map/all_to_all | solution.py:216
  217.1 5.8 %all-to-all-start.3 = ((f32[8,2,1024]{2,1,0:T(2,128)}), f32[8,2,1024]{2,1,0:T(2,128)S(1)}, u32[]{:S(2)}, u32[]{:S(2)}) async-start(f32[8,2,1024]{2,1,0:T(2,128)} %broadcast_in_dim.38), calls=%async_computation.3 | async-start | bytes 131072 | tf_op jit(solution)/shard_map/all_to_all | solution.py:216
  223.0 6.5 %all-to-all-done.3 = f32[8,2,1024]{2,1,0:T(2,128)S(1)} async-done(((f32[8,2,1024]{2,1,0:T(2,128)}), f32[8,2,1024]{2,1,0:T(2,128)S(1)}, u32[]{:S(2)}, u32[]{:S(2)}) %all-to-all-start.3) | async-done | bytes 65568 | tf_op jit(solution)/shard_map/all_to_all | solution.py:216
  230.6 7.3 %output.1 = f32[512,4,640]{2,1,0:T(4,128)} custom-call(s32[512]{0:T(512)S(1)} %reshape.285.order, s32[4]{0:T(128)S(1)} %pad_add_fusion.place, f32[4,4,4,16,640]{4,3,2,1,0:T(8,128)} %bitcast.95, f32[4,4,4,16,640]{4,3,2,1,0:T(8,128)} %bitcast.46.other, f32[16,8,16,1]{3,2,1,0:T(8,128)S(1)} %copy.103.totals), custom_call_target="tpu_custom_call" | custom-call | tf_op jit(solution)/shard_map/output/pallas_call | solution.py:180
  (150 shorter events, 42.7 us)
Async XLA Ops:
  14.6 15.1 %all-to-all-start = ((bf16[16,8,1408]{2,1,0:T(8,128)(2,1)}), bf16[16,8,1408]{2,1,0:T(8,128)(2,1)S(1)}, u32[]{:S(2)}, u32[]{:S(2)}) async-start(bf16[16,8,1408]{2,1,0:T(8,128)(2,1)} %fusion.2), calls=%async_computation | async-start | bytes 720896 | tf_op jit(solution)/shard_map/all_to_all | solution.py:272
  42.8 35.6 %all-to-all-start.1 = ((f32[4,32,5120]{2,1,0:T(8,128)}), f32[4,32,5120]{2,1,0:T(8,128)}, u32[]{:S(2)}, u32[]{:S(2)}) async-start(f32[4,32,5120]{2,1,0:T(8,128)} %bitcast.94), calls=%async_computation.1 | async-start | bytes 5242880 | tf_op jit(solution)/shard_map/all_to_all | solution.py:303
  80.3 9.5 %collective-permute-start = (f32[16,5120]{1,0:T(8,128)S(1)}, f32[16,5120]{1,0:T(8,128)S(1)}, u32[]{:S(2)}, u32[]{:S(2)}) collective-permute-start(f32[16,5120]{1,0:T(8,128)S(1)} %get-tuple-element.11), channel_id=1, source_target_pairs={{0,1},{1,0},{2,3},{3,2},{4,5},{5,4},{6,7},{7,6},{8,9},{9,8},{10,11... | collective-permute-start | bytes 983048 | tf_op jit(solution)/shard_map/ppermute | solution.py:308
  83.7 87.9 %collective-permute-start.28 = (bf16[5120,640]{1,0:T(8,128)(2,1)}, bf16[5120,640]{1,0:T(8,128)(2,1)}, u32[]{:S(2)}, u32[]{:S(2)}) collective-permute-start(bf16[5120,640]{1,0:T(8,128)(2,1)} %refs_12_.1), channel_id=1, source_target_pairs={{0,8},{1,9},{2,10},{3,11},{4,12},{5,13},{6,14},{7,15},{8,0},{9,1},... | collective-permute-start | bytes 19660808 | tf_op jit(solution)/shard_map/ppermute | solution.py:51
  90.1 5.3 %collective-permute-start.1 = (bf16[16,1792]{1,0:T(8,128)(2,1)S(1)}, bf16[16,1792]{1,0:T(8,128)(2,1)S(1)}, u32[]{:S(2)}, u32[]{:S(2)}) collective-permute-start(bf16[16,1792]{1,0:T(8,128)(2,1)S(1)} %get-tuple-element.33), channel_id=1, source_target_pairs={{0,16},{1,17},{2,18},{3,19},{4,20},{5,21},{6,22},{7,23},{8,56},{9,... | collective-permute-start | bytes 172040 | tf_op jit(solution)/shard_map/ppermute | solution.py:60
  94.1 5.2 %collective-permute-start.10 = (bf16[16,1792]{1,0:T(8,128)(2,1)S(1)}, bf16[16,1792]{1,0:T(8,128)(2,1)S(1)}, u32[]{:S(2)}, u32[]{:S(2)}) collective-permute-start(bf16[16,1792]{1,0:T(8,128)(2,1)S(1)} %get-tuple-element.32), channel_id=1, source_target_pairs={{0,2},{1,3},{2,4},{3,5},{4,6},{5,7},{6,0},{7,1},{8,14},{9,15},{10,... | collective-permute-start | bytes 172040 | tf_op jit(solution)/shard_map/ppermute | solution.py:60
  95.4 4.8 %collective-permute-start.2 = (bf16[16,1792]{1,0:T(8,128)(2,1)S(1)}, bf16[16,1792]{1,0:T(8,128)(2,1)S(1)}, u32[]{:S(2)}, u32[]{:S(2)}) collective-permute-start(bf16[16,1792]{1,0:T(8,128)(2,1)S(1)} %collective-permute-done.1), channel_id=1, source_target_pairs={{0,16},{1,17},{2,18},{3,19},{4,20},{5,21},{6,22},{7,23},{8,56},{9,... | collective-permute-start | bytes 172040 | tf_op jit(solution)/shard_map/ppermute | solution.py:60
  98.4 4.2 %collective-permute-start.19 = (bf16[16,1536]{1,0:T(8,128)(2,1)S(1)}, bf16[16,1536]{1,0:T(8,128)(2,1)S(1)}, u32[]{:S(2)}, u32[]{:S(2)}) collective-permute-start(bf16[16,1536]{1,0:T(8,128)(2,1)S(1)} %get-tuple-element.29), channel_id=1, source_target_pairs={{0,64},{1,65},{2,66},{3,67},{4,68},{5,69},{6,70},{7,71},{8,73},{9,... | collective-permute-start | bytes 147464 | tf_op jit(solution)/shard_map/ppermute | solution.py:60
  99.3 8.6 %collective-permute-start.11 = (bf16[16,1792]{1,0:T(8,128)(2,1)S(1)}, bf16[16,1792]{1,0:T(8,128)(2,1)S(1)}, u32[]{:S(2)}, u32[]{:S(2)}) collective-permute-start(bf16[16,1792]{1,0:T(8,128)(2,1)S(1)} %collective-permute-done.10), channel_id=1, source_target_pairs={{0,2},{1,3},{2,4},{3,5},{4,6},{5,7},{6,0},{7,1},{8,14},{9,15},{10,... | collective-permute-start | bytes 172040 | tf_op jit(solution)/shard_map/ppermute | solution.py:60
  100.2 8.3 %collective-permute-start.3 = (bf16[16,1792]{1,0:T(8,128)(2,1)S(1)}, bf16[16,1792]{1,0:T(8,128)(2,1)S(1)}, u32[]{:S(2)}, u32[]{:S(2)}) collective-permute-start(bf16[16,1792]{1,0:T(8,128)(2,1)S(1)} %collective-permute-done.2), channel_id=1, source_target_pairs={{0,16},{1,17},{2,18},{3,19},{4,20},{5,21},{6,22},{7,23},{8,56},{9,... | collective-permute-start | bytes 172040 | tf_op jit(solution)/shard_map/ppermute | solution.py:60
  105.6 9.7 %collective-permute-start.21 = (bf16[16,1536]{1,0:T(8,128)(2,1)S(1)}, bf16[16,1536]{1,0:T(8,128)(2,1)S(1)}, u32[]{:S(2)}, u32[]{:S(2)}) collective-permute-start(bf16[16,1536]{1,0:T(8,128)(2,1)S(1)} %collective-permute-done.20), channel_id=1, source_target_pairs={{0,64},{1,65},{2,66},{3,67},{4,68},{5,69},{6,70},{7,71},{8,73},{9,... | collective-permute-start | bytes 147464 | tf_op jit(solution)/shard_map/ppermute | solution.py:60
  108.6 5.2 %collective-permute-start.4 = (bf16[4,16,1792]{2,1,0:T(8,128)(2,1)S(1)}, bf16[4,16,1792]{2,1,0:T(8,128)(2,1)S(1)}, u32[]{:S(2)}, u32[]{:S(2)}) collective-permute-start(bf16[4,16,1792]{2,1,0:T(8,128)(2,1)S(1)} %get-tuple-element.25), channel_id=1, source_target_pairs={{0,2},{1,3},{2,4},{3,5},{4,6},{5,7},{6,0},{7,1},{8,14},{9,15},{10,... | collective-permute-start | bytes 688136 | tf_op jit(solution)/shard_map/ppermute | solution.py:60
  111.0 5.2 %collective-permute-start.13 = (bf16[4,16,1792]{2,1,0:T(8,128)(2,1)S(1)}, bf16[4,16,1792]{2,1,0:T(8,128)(2,1)S(1)}, u32[]{:S(2)}, u32[]{:S(2)}) collective-permute-start(bf16[4,16,1792]{2,1,0:T(8,128)(2,1)S(1)} %get-tuple-element.23), channel_id=1, source_target_pairs={{0,64},{1,65},{2,66},{3,67},{4,68},{5,69},{6,70},{7,71},{8,73},{9,... | collective-permute-start | bytes 688136 | tf_op jit(solution)/shard_map/ppermute | solution.py:60
  113.8 4.9 %collective-permute-start.5 = (bf16[4,16,1792]{2,1,0:T(8,128)(2,1)S(1)}, bf16[4,16,1792]{2,1,0:T(8,128)(2,1)S(1)}, u32[]{:S(2)}, u32[]{:S(2)}) collective-permute-start(bf16[4,16,1792]{2,1,0:T(8,128)(2,1)S(1)} %collective-permute-done.4), channel_id=1, source_target_pairs={{0,2},{1,3},{2,4},{3,5},{4,6},{5,7},{6,0},{7,1},{8,14},{9,15},{10,... | collective-permute-start | bytes 688136 | tf_op jit(solution)/shard_map/ppermute | solution.py:60
  115.3 6.1 %collective-permute-start.22 = (bf16[4,16,1536]{2,1,0:T(8,128)(2,1)S(1)}, bf16[4,16,1536]{2,1,0:T(8,128)(2,1)S(1)}, u32[]{:S(2)}, u32[]{:S(2)}) collective-permute-start(bf16[4,16,1536]{2,1,0:T(8,128)(2,1)S(1)} %get-tuple-element.27), channel_id=1, source_target_pairs={{0,16},{1,17},{2,18},{3,19},{4,20},{5,21},{6,22},{7,23},{8,56},{9,... | collective-permute-start | bytes 589832 | tf_op jit(solution)/shard_map/ppermute | solution.py:60
  116.3 10.9 %collective-permute-start.14 = (bf16[4,16,1792]{2,1,0:T(8,128)(2,1)S(1)}, bf16[4,16,1792]{2,1,0:T(8,128)(2,1)S(1)}, u32[]{:S(2)}, u32[]{:S(2)}) collective-permute-start(bf16[4,16,1792]{2,1,0:T(8,128)(2,1)S(1)} %collective-permute-done.13), channel_id=1, source_target_pairs={{0,64},{1,65},{2,66},{3,67},{4,68},{5,69},{6,70},{7,71},{8,73},{9,... | collective-permute-start | bytes 688136 | tf_op jit(solution)/shard_map/ppermute | solution.py:60
  118.7 9.5 %collective-permute-start.6 = (bf16[4,16,1792]{2,1,0:T(8,128)(2,1)S(1)}, bf16[4,16,1792]{2,1,0:T(8,128)(2,1)S(1)}, u32[]{:S(2)}, u32[]{:S(2)}) collective-permute-start(bf16[4,16,1792]{2,1,0:T(8,128)(2,1)S(1)} %collective-permute-done.5), channel_id=1, source_target_pairs={{0,2},{1,3},{2,4},{3,5},{4,6},{5,7},{6,0},{7,1},{8,14},{9,15},{10,... | collective-permute-start | bytes 688136 | tf_op jit(solution)/shard_map/ppermute | solution.py:60
  121.4 4.5 %collective-permute-start.23 = (bf16[4,16,1536]{2,1,0:T(8,128)(2,1)S(1)}, bf16[4,16,1536]{2,1,0:T(8,128)(2,1)S(1)}, u32[]{:S(2)}, u32[]{:S(2)}) collective-permute-start(bf16[4,16,1536]{2,1,0:T(8,128)(2,1)S(1)} %collective-permute-done.22), channel_id=1, source_target_pairs={{0,16},{1,17},{2,18},{3,19},{4,20},{5,21},{6,22},{7,23},{8,56},{9,... | collective-permute-start | bytes 589832 | tf_op jit(solution)/shard_map/ppermute | solution.py:60
  125.9 6.6 %collective-permute-start.24 = (bf16[4,16,1536]{2,1,0:T(8,128)(2,1)S(1)}, bf16[4,16,1536]{2,1,0:T(8,128)(2,1)S(1)}, u32[]{:S(2)}, u32[]{:S(2)}) collective-permute-start(bf16[4,16,1536]{2,1,0:T(8,128)(2,1)S(1)} %collective-permute-done.23), channel_id=1, source_target_pairs={{0,16},{1,17},{2,18},{3,19},{4,20},{5,21},{6,22},{7,23},{8,56},{9,... | collective-permute-start | bytes 589832 | tf_op jit(solution)/shard_map/ppermute | solution.py:60
  127.2 4.9 %collective-permute-start.15 = (bf16[4,16,1792]{2,1,0:T(8,128)(2,1)S(1)}, bf16[4,16,1792]{2,1,0:T(8,128)(2,1)S(1)}, u32[]{:S(2)}, u32[]{:S(2)}) collective-permute-start(bf16[4,16,1792]{2,1,0:T(8,128)(2,1)S(1)} %collective-permute-done.14), channel_id=1, source_target_pairs={{0,64},{1,65},{2,66},{3,67},{4,68},{5,69},{6,70},{7,71},{8,73},{9,... | collective-permute-start | bytes 688136 | tf_op jit(solution)/shard_map/ppermute | solution.py:60
  128.4 13.8 %collective-permute-start.7 = (bf16[4,4,16,1792]{3,2,1,0:T(8,128)(2,1)S(1)}, bf16[4,4,16,1792]{3,2,1,0:T(8,128)(2,1)S(1)}, u32[]{:S(2)}, u32[]{:S(2)}) collective-permute-start(bf16[4,4,16,1792]{3,2,1,0:T(8,128)(2,1)S(1)} %pad_maximum_fusion.refs_0_), channel_id=1, source_target_pairs={{0,64},{1,65},{2,66},{3,67},{4,68},{5,69},{6,70},{7,71},{8,73},{9,... | collective-permute-start | bytes 2752520 | tf_op jit(solution)/shard_map/ppermute | solution.py:60
  132.2 12.6 %collective-permute-start.16 = (bf16[4,4,16,1792]{3,2,1,0:T(8,128)(2,1)S(1)}, bf16[4,4,16,1792]{3,2,1,0:T(8,128)(2,1)S(1)}, u32[]{:S(2)}, u32[]{:S(2)}) collective-permute-start(bf16[4,4,16,1792]{3,2,1,0:T(8,128)(2,1)S(1)} %pad_maximum_fusion.1.refs_4_), channel_id=1, source_target_pairs={{0,16},{1,17},{2,18},{3,19},{4,20},{5,21},{6,22},{7,23},{8,56},{9,... | collective-permute-start | bytes 2752520 | tf_op jit(solution)/shard_map/ppermute | solution.py:60
  132.6 13.6 %collective-permute-start.25 = (bf16[4,4,16,1536]{3,2,1,0:T(8,128)(2,1)S(1)}, bf16[4,4,16,1536]{3,2,1,0:T(8,128)(2,1)S(1)}, u32[]{:S(2)}, u32[]{:S(2)}) collective-permute-start(bf16[4,4,16,1536]{3,2,1,0:T(8,128)(2,1)S(1)} %pad_maximum_fusion.2.refs_8_), channel_id=1, source_target_pairs={{0,2},{1,3},{2,4},{3,5},{4,6},{5,7},{6,0},{7,1},{8,14},{9,15},{10,... | collective-permute-start | bytes 2359304 | tf_op jit(solution)/shard_map/ppermute | solution.py:60
  142.2 12.6 %collective-permute-start.8 = (bf16[4,4,16,1792]{3,2,1,0:T(8,128)(2,1)S(1)}, bf16[4,4,16,1792]{3,2,1,0:T(8,128)(2,1)}, u32[]{:S(2)}, u32[]{:S(2)}) collective-permute-start(bf16[4,4,16,1792]{3,2,1,0:T(8,128)(2,1)S(1)} %collective-permute-done.7.refs_1_), channel_id=1, source_target_pairs={{0,64},{1,65},{2,66},{3,67},{4,68},{5,69},{6,70},{7,71},{8,73},{9,... | collective-permute-start | bytes 2752520 | tf_op jit(solution)/shard_map/ppermute | solution.py:60
  144.8 13.0 %collective-permute-start.17 = (bf16[4,4,16,1792]{3,2,1,0:T(8,128)(2,1)S(1)}, bf16[4,4,16,1792]{3,2,1,0:T(8,128)(2,1)}, u32[]{:S(2)}, u32[]{:S(2)}) collective-permute-start(bf16[4,4,16,1792]{3,2,1,0:T(8,128)(2,1)S(1)} %collective-permute-done.16.refs_5_), channel_id=1, source_target_pairs={{0,16},{1,17},{2,18},{3,19},{4,20},{5,21},{6,22},{7,23},{8,56},{9,... | collective-permute-start | bytes 2752520 | tf_op jit(solution)/shard_map/ppermute | solution.py:60
  146.3 13.9 %collective-permute-start.26 = (bf16[4,4,16,1536]{3,2,1,0:T(8,128)(2,1)S(1)}, bf16[4,4,16,1536]{3,2,1,0:T(8,128)(2,1)}, u32[]{:S(2)}, u32[]{:S(2)}) collective-permute-start(bf16[4,4,16,1536]{3,2,1,0:T(8,128)(2,1)S(1)} %collective-permute-done.25.refs_9_), channel_id=1, source_target_pairs={{0,2},{1,3},{2,4},{3,5},{4,6},{5,7},{6,0},{7,1},{8,14},{9,15},{10,... | collective-permute-start | bytes 2359304 | tf_op jit(solution)/shard_map/ppermute | solution.py:60
  154.8 16.8 %collective-permute-start.9 = (bf16[4,4,16,1792]{3,2,1,0:T(8,128)(2,1)}, bf16[4,4,16,1792]{3,2,1,0:T(8,128)(2,1)}, u32[]{:S(2)}, u32[]{:S(2)}) collective-permute-start(bf16[4,4,16,1792]{3,2,1,0:T(8,128)(2,1)} %collective-permute-done.8.refs_2_), channel_id=1, source_target_pairs={{0,64},{1,65},{2,66},{3,67},{4,68},{5,69},{6,70},{7,71},{8,73},{9,... | collective-permute-start | bytes 2752520 | tf_op jit(solution)/shard_map/ppermute | solution.py:60
  157.7 13.9 %collective-permute-start.18 = (bf16[4,4,16,1792]{3,2,1,0:T(8,128)(2,1)}, bf16[4,4,16,1792]{3,2,1,0:T(8,128)(2,1)}, u32[]{:S(2)}, u32[]{:S(2)}) collective-permute-start(bf16[4,4,16,1792]{3,2,1,0:T(8,128)(2,1)} %collective-permute-done.17.refs_6_), channel_id=1, source_target_pairs={{0,16},{1,17},{2,18},{3,19},{4,20},{5,21},{6,22},{7,23},{8,56},{9,... | collective-permute-start | bytes 2752520 | tf_op jit(solution)/shard_map/ppermute | solution.py:60
  160.1 11.5 %collective-permute-start.27 = (bf16[4,4,16,1536]{3,2,1,0:T(8,128)(2,1)}, bf16[4,4,16,1536]{3,2,1,0:T(8,128)(2,1)}, u32[]{:S(2)}, u32[]{:S(2)}) collective-permute-start(bf16[4,4,16,1536]{3,2,1,0:T(8,128)(2,1)} %collective-permute-done.26.refs_10_), channel_id=1, source_target_pairs={{0,2},{1,3},{2,4},{3,5},{4,6},{5,7},{6,0},{7,1},{8,14},{9,15},{10,... | collective-permute-start | bytes 2359304 | tf_op jit(solution)/shard_map/ppermute | solution.py:60
  193.1 37.6 %collective-permute-start.29 = (f32[1024,640]{1,0:T(8,128)}, f32[1024,640]{1,0:T(8,128)}, u32[]{:S(2)}, u32[]{:S(2)}) collective-permute-start(f32[1024,640]{1,0:T(8,128)} %get-tuple-element.10), channel_id=1, source_target_pairs={{0,8},{1,9},{2,10},{3,11},{4,12},{5,13},{6,14},{7,15},{8,0},{9,1},... | collective-permute-start | bytes 7864328 | tf_op jit(solution)/shard_map/ppermute | solution.py:51
  207.0 9.2 %all-to-all-start.2 = ((f32[16,1,1056]{2,1,0:T(1,128)}), f32[16,1,1056]{2,1,0:T(1,128)S(1)}, u32[]{:S(2)}, u32[]{:S(2)}) async-start(f32[16,1,1056]{2,1,0:T(1,128)} %broadcast_in_dim.37), calls=%async_computation.2 | async-start | bytes 147456 | tf_op jit(solution)/shard_map/all_to_all | solution.py:216
  217.1 12.5 %all-to-all-start.3 = ((f32[8,2,1024]{2,1,0:T(2,128)}), f32[8,2,1024]{2,1,0:T(2,128)S(1)}, u32[]{:S(2)}, u32[]{:S(2)}) async-start(f32[8,2,1024]{2,1,0:T(2,128)} %broadcast_in_dim.38), calls=%async_computation.3 | async-start | bytes 131072 | tf_op jit(solution)/shard_map/all_to_all | solution.py:216
  (19 other events, 214.5 us)
